TPU v7x, 32 devices: a whole 2x2x4 slice. The times are simulated.
32 devices in a mesh: tm: 8 (over z, x), chan: 4 (over y, core).
Axes of the slice: x: 2, y: 2, z: 4, core: 2. Of those that a mesh axis runs over, the one named last changes fastest.
Arguments:
- record: bfloat16 [98304, 512], P('tm', 'chan')
- window_starts: int32 [32], P('tm'), may hold values from 0 to 86016, as said below
- alive_mask: int32 [512], P('chan'), may hold values 0 or 1
Outputs:
- stacked: float32 [2, 288, 512, 512], P(None, 'tm', 'chan')
Inputs may be any that keep to these rules, and one draw needn't show every extreme that they name: `window_starts`: window k starts at a sample of k // 4 * 12288 to (k // 4 + 1) * 12288 - 1, and every window ends inside the record.
All inputs are finite; a program needn't handle non-finite values. No bound on the sum of `alive_mask` on one device may be relied on, other than what follows from the above.
Results may differ from a plain program's by a relative error of at most 0.0037.
Values may be sent and summed in bfloat16 or wider, within the bound.
A program may use at most 320 MiB of HBM per device.

v0:
```python
import math

import jax
import jax.numpy as jnp
from jax import lax
from jax.sharding import PartitionSpec as P

KEEP = 288
FLO = 61
HALF = 32
BAND = 512
WPD = 4


epsilon = 1e-06


def passed_along(block, axis, distance):
    devices = range(lax.axis_size(axis))
    route = [(i - distance, i) for i in devices if i - distance in devices]
    return lax.ppermute(block, axis, route)


def build_tables(window_length):
    bin_count = KEEP + 2 * HALF
    block_length = math.gcd(window_length, 2048)
    step_angle = 2.0 * math.pi / window_length
    bin_numbers = FLO - HALF + lax.iota(jnp.int32, bin_count)
    base_times = lax.iota(jnp.int32, block_length)
    base_phases = bin_numbers[:, None] * base_times[None, :] % window_length
    base_angles = step_angle * base_phases.astype(jnp.float32)
    base_cos = jnp.cos(base_angles)
    base_sin = jnp.sin(base_angles)
    tables = []
    for first_time in range(0, window_length, block_length):
        shift_phases = bin_numbers * first_time % window_length
        shift_angles = step_angle * shift_phases.astype(jnp.float32)
        shift_cos = jnp.cos(shift_angles)[:, None]
        shift_sin = jnp.sin(shift_angles)[:, None]
        sample_times = (first_time + base_times).astype(jnp.float32)
        tapering = (0.5 - 0.5 * jnp.cos(step_angle * sample_times))[None, :]
        cos_values = base_cos * shift_cos - base_sin * shift_sin
        sin_values = base_sin * shift_cos + base_cos * shift_sin
        cosine = (tapering * cos_values).astype(jnp.bfloat16)
        sine_rows = (-tapering * sin_values).astype(jnp.bfloat16)
        tables.append(jnp.concatenate([cosine, sine_rows], 0))
    return (tables, block_length)


def smoother_matrix():
    row_index = lax.iota(jnp.int32, KEEP)[:, None]
    column_index = lax.iota(jnp.int32, KEEP + 2 * HALF)[None, :]
    inside = (column_index >= row_index) & (column_index <= row_index + 2 * HALF)
    return inside.astype(jnp.float32)


def whiten(spectra, alive_mask):
    bin_count = KEEP + 2 * HALF
    real_part = spectra[:, :bin_count]
    imag_part = spectra[:, bin_count:]
    magnitude = jnp.sqrt(real_part * real_part + imag_part * imag_part)
    smoothed = jnp.einsum(
        "kj,wjc->wkc", smoother_matrix(), magnitude, precision=lax.Precision.HIGHEST
    ) / (2 * HALF + 1)
    scaling = alive_mask.astype(jnp.float32)[None, None, :] / (smoothed + epsilon)
    white_real = real_part[:, HALF : HALF + KEEP] * scaling
    white_imag = imag_part[:, HALF : HALF + KEEP] * scaling
    whitened = jnp.stack([white_real, white_imag], 2).astype(jnp.bfloat16)
    return jnp.transpose(whitened, (1, 0, 2, 3))


def transform(frames, tables, block_length):
    bin_count = KEEP + 2 * HALF
    totals = jnp.zeros((frames.shape[0], 2 * bin_count, frames.shape[2]), jnp.float32)
    for number, lookup in enumerate(tables):
        first_time = number * block_length
        segment = frames[:, first_time : first_time + block_length]
        totals = totals + jnp.einsum(
            "ft,wtc->wfc", lookup, segment, preferred_element_type=jnp.float32
        )
    return totals


def band_rows(gram, band_width):
    row_count = gram.shape[-2]

    def pick(rows, start):
        return lax.dynamic_slice_in_dim(rows, start, band_width, rows.ndim - 1)

    starts = lax.iota(jnp.int32, row_count)
    return jax.vmap(pick, in_axes=(gram.ndim - 2, 0), out_axes=gram.ndim - 2)(gram, starts)


def local(record, window_starts, alive_mask):
    window_length = record.shape[0]
    local_width = record.shape[1]
    tables, block_length = build_tables(window_length)
    index_time = lax.axis_index("tm")
    offsets = window_starts - index_time * window_length
    following = passed_along(record, "tm", -1)
    joined = jnp.concatenate([record, following], 0)
    frames = jnp.stack(
        [
            lax.dynamic_slice_in_dim(joined, offsets[number], window_length, 0)
            for number in range(WPD)
        ]
    )
    spectra = transform(frames, tables, block_length)
    whitened = whiten(spectra, alive_mask)
    regrouped = lax.all_to_all(whitened, "tm", split_axis=0, concat_axis=1, tiled=True)
    reach_count = BAND // local_width
    pieces = [regrouped]
    for distance in range(1, reach_count + 1):
        pieces.append(passed_along(regrouped, "chan", -distance))
    extended = jnp.concatenate(pieces, 3)
    blocks = jnp.einsum("fwrc,fwsj->frscj", regrouped, extended, preferred_element_type=jnp.float32)
    real_gram = blocks[:, 0, 0] + blocks[:, 1, 1]
    imag_gram = blocks[:, 1, 0] - blocks[:, 0, 1]
    both = jnp.stack([real_gram, imag_gram], 0)
    return band_rows(both, BAND) / regrouped.shape[1]


def solution(mesh):
    return jax.shard_map(
        local,
        mesh=mesh,
        in_specs=(P("tm", "chan"), P("tm"), P("chan")),
        out_specs=P(None, "tm", "chan", None),
        check_vma=False,
    )
```

profile of v0, /device:TPU:0, one launch (start us, length us, event | category | flops | bytes accessed | tf_op | source)
XLA Modules:
  0.0 429.6 jit_solution(1146710627107403253)
XLA Ops:
  11.8 12.9 %multiply_convert_fusion.9 = (bf16[352,2048]{1,0:T(8,128)(2,1)S(1)}, bf16[352,2048]{1,0:T(8,128)(2,1)S(1)}) fusion(f32[352]{0:T(512)S(1)} %get-tuple-element.53, f32[352]{0:T(512)S(1)} %get-tuple-element.54, f32[2048]{0:T(1024)S(1)} %get-tuple-element.51, s32[352]{0:T(512)S(1)} %iota_add_fusion.1, f32[2048]{0:T(1024)S(1)} %get-tuple-element.52), kind=kLoop, calls=%fused_computation.52 | loop fusion | flops 13697024 | bytes 2904192 | tf_op jit(solution)/shard_map/convert_element_type | solution.py:44
  24.8 18.6 %multiply_convert_fusion.1 = (bf16[352,2048]{1,0:T(8,128)(2,1)S(1)}, bf16[352,2048]{1,0:T(8,128)(2,1)S(1)}, bf16[352,2048]{1,0:T(8,128)(2,1)}, bf16[352,2048]{1,...) fusion(f32[352]{0:T(512)S(1)} %get-tuple-element.43, ...), kind=kLoop, calls=%fused_computation.44 | loop fusion | flops 41091072 | bytes 14512512 | tf_op jit(solution)/shard_map/convert_element_type | solution.py:44
  43.6 29.6 %collective-permute-done = bf16[12288,128]{1,0:T(8,128)(2,1)S(1)} collective-permute-done((bf16[12288,128]{1,0:T(8,128)(2,1)}, bf16[12288,128]{1,0:T(8,128)(2,1)S(1)}, u32[]{:S(2)}, u32[]{:S(2)}) %collective-permute-start) | collective-permute-done | bytes 3145760 | tf_op jit(solution)/shard_map/ppermute | solution.py:21
  73.6 3.3 dynamic-slice_bitcast_fusion.3
  76.9 1.8 pad_maximum_fusion
  78.8 1.7 fusion.9
  80.6 1.7 fusion.18
  82.4 1.7 fusion.15
  84.1 1.7 fusion.12
  85.9 1.7 fusion.6
  87.6 2.0 add_bitcast_fusion
  91.0 21.4 %all_to_all.18 = bf16[288,4,2,128]{3,1,2,0:T(4,128)(2,1)S(1)} all-to-all(bf16[288,4,2,128]{3,1,2,0:T(4,128)(2,1)S(1)} %copy.15), channel_id=1, replica_groups=mesh['tm'=8,'chan'=4] {'tm'}, dimensions={0} | all-to-all | bytes 1179648 | tf_op jit(solution)/shard_map/all_to_all | solution.py:110
  113.3 1.3 collective-permute-start.1
  114.6 1.3 collective-permute-start.2
  118.2 23.3 %collective-permute-done.2 = bf16[36,32,2,128]{3,1,2,0:T(8,128)(2,1)S(1)} collective-permute-done((bf16[36,32,2,128]{3,1,2,0:T(8,128)(2,1)S(1)}, bf16[36,32,2,128]{3,1,2,0:T(8,128)(2,1)S(1)}, u32[]{:S(2)}, u32[]{:S(2)}) %collective-permute-start.2) | collective-permute-done | bytes 589856 | tf_op jit(solution)/shard_map/ppermute | solution.py:21
  141.7 1.9 collective-permute-done.3
  143.9 18.4 %convolution_bitcast_fusion = f32[36,2,2,128,640]{3,4,1,2,0:T(8,128)} fusion(bf16[36,32,2,128,1]{3,1,2,4,0:T(8,128)(2,1)S(1)} %bitcast.88, bf16[36,32,2,640]{3,1,2,0:T(8,128)(2,1)S(1)} %constant_dynamic-update-slice_fusion.2), kind=kOutput, calls=%fused_computation.3 | convolution fusion | flops 754974720 | bytes 50724864 | tf_op jit(solution)/shard_map/fwrc,fwsj->frscj/dot_general | solution.py:116
  162.3 8.5 %fusion = f32[1,36,128,640]{2,3,1,0:T(8,128)S(1)} fusion(f32[36,2,2,128,640]{3,4,1,2,0:T(8,128)} %convolution_bitcast_fusion), kind=kLoop, calls=%fused_computation.6 | loop fusion | flops 2949120 | bytes 35389440 | tf_op jit(solution)/shard_map/sub | solution.py:118
  170.8 8.5 %fusion.2 = f32[1,36,128,640]{2,3,1,0:T(8,128)S(1)} fusion(f32[36,2,2,128,640]{3,4,1,2,0:T(8,128)} %convolution_bitcast_fusion), kind=kLoop, calls=%fused_computation.9 | loop fusion | flops 2949120 | bytes 35389440 | tf_op jit(solution)/shard_map/add | solution.py:117
  179.3 8.2 %maximum_bitcast_fusion = f32[128,2,36,640]{0,3,2,1:T(8,128)} fusion(f32[1,36,128,640]{2,3,1,0:T(8,128)S(1)} %fusion, f32[1,36,128,640]{2,3,1,0:T(8,128)S(1)} %fusion.2), kind=kLoop, calls=%fused_computation.2 | loop fusion | flops 5898240 | bytes 47185920 | tf_op jit(solution)/shard_map/vmap()/transpose | solution.py:88
  187.4 68.7 %copy.20 = f32[128,2,36,640]{2,1,0,3:T(2,128)} copy(f32[128,2,36,640]{0,3,2,1:T(8,128)} %maximum_bitcast_fusion) | data formatting | bytes 47185920 | tf_op jit(solution)/shard_map/vmap()/transpose | solution.py:88
  256.2 72.6 %gather_fusion = f32[128,2,36,512]{2,1,3,0:T(2,128)} fusion(f32[128,2,36,640]{2,1,0,3:T(2,128)} %copy.20, s32[128]{0:T(128)S(1)} %iota_multiply_fusion), kind=kCustom, calls=%fused_computation | custom fusion | bytes 37750784 | tf_op jit(solution)/shard_map/vmap()/gather | solution.py:88
  328.8 43.6 %multiply_bitcast_fusion = f32[2,36,128,512]{1,0,3,2:T(2,128)} fusion(f32[128,2,36,512]{2,1,3,0:T(2,128)} %gather_fusion), kind=kLoop, calls=%fused_computation.1 | loop fusion | flops 4718592 | bytes 37748736 | tf_op jit(solution)/shard_map/div | solution.py:120
  372.4 57.2 %copy.21 = f32[2,36,128,512]{3,2,1,0:T(8,128)} copy(f32[2,36,128,512]{1,0,3,2:T(2,128)} %multiply_bitcast_fusion) | data formatting | bytes 37748736 | tf_op jit(solution)/shard_map/div | solution.py:120
  (52 shorter events, 10.1 us)
Async XLA Ops:
  0.0 73.1 %collective-permute-start = (bf16[12288,128]{1,0:T(8,128)(2,1)}, bf16[12288,128]{1,0:T(8,128)(2,1)S(1)}, u32[]{:S(2)}, u32[]{:S(2)}) collective-permute-start(bf16[12288,128]{1,0:T(8,128)(2,1)} %param.3), channel_id=1, source_target_pairs={{4,0},{8,4},{12,8},{16,12},{20,16},{24,20},{28,24},{5,1},{9,5},{13... | collective-permute-start | bytes 9437192 | tf_op jit(solution)/shard_map/ppermute | solution.py:21
  24.7 18.6 %copy-start = (bf16[12288,128]{1,0:T(8,128)(2,1)S(1)}, bf16[12288,128]{1,0:T(8,128)(2,1)}, u32[]{:S(2)}) copy-start(bf16[12288,128]{1,0:T(8,128)(2,1)} %param.3) | copy-start | bytes 9437188
  78.7 1.7 copy-start.7
  78.8 1.8 copy-start.8
  80.5 1.7 copy-start.5
  80.6 1.8 copy-start.6
  82.3 1.7 copy-start.3
  82.3 1.8 copy-start.4
  84.1 1.7 copy-start.1
  84.1 1.8 copy-start.2
  113.3 4.7 %collective-permute-start.1 = (bf16[36,32,2,128]{3,1,2,0:T(8,128)(2,1)S(1)}, bf16[36,32,2,128]{3,1,2,0:T(8,128)(2,1)S(1)}, u32[]{:S(2)}, u32[]{:S(2)}) collective-permute-start(bf16[36,32,2,128]{3,1,2,0:T(8,128)(2,1)S(1)} %bitcast.83), channel_id=1, source_target_pairs={{1,0},{2,1},{3,2},{5,4},{6,5},{7,6},{9,8},{10,9},{11,10},{13,12},{... | collective-permute-start | bytes 1769480 | tf_op jit(solution)/shard_map/ppermute | solution.py:21
  114.6 26.9 %collective-permute-start.2 = (bf16[36,32,2,128]{3,1,2,0:T(8,128)(2,1)S(1)}, bf16[36,32,2,128]{3,1,2,0:T(8,128)(2,1)S(1)}, u32[]{:S(2)}, u32[]{:S(2)}) collective-permute-start(bf16[36,32,2,128]{3,1,2,0:T(8,128)(2,1)S(1)} %bitcast.84), channel_id=1, source_target_pairs={{2,0},{3,1},{6,4},{7,5},{10,8},{11,9},{14,12},{15,13},{18,16},{19,... | collective-permute-start | bytes 1769480 | tf_op jit(solution)/shard_map/ppermute | solution.py:21
  115.9 27.6 %collective-permute-start.3 = (bf16[36,32,2,128]{3,1,2,0:T(8,128)(2,1)S(1)}, bf16[36,32,2,128]{3,1,2,0:T(8,128)(2,1)S(1)}, u32[]{:S(2)}, u32[]{:S(2)}) collective-permute-start(bf16[36,32,2,128]{3,1,2,0:T(8,128)(2,1)S(1)} %bitcast.85), channel_id=1, source_target_pairs={{3,0},{7,4},{11,8},{15,12},{19,16},{23,20},{27,24},{31,28}} | collective-permute-start | bytes 1769480 | tf_op jit(solution)/shard_map/ppermute | solution.py:21
  117.2 26.5 %collective-permute-start.4 = (bf16[36,32,2,128]{3,1,2,0:T(8,128)(2,1)S(1)}, bf16[36,32,2,128]{3,1,2,0:T(8,128)(2,1)S(1)}, u32[]{:S(2)}, u32[]{:S(2)}) collective-permute-start(bf16[36,32,2,128]{3,1,2,0:T(8,128)(2,1)S(1)} %bitcast.86), channel_id=1, source_target_pairs={} | collective-permute-start | bytes 1769480 | tf_op jit(solution)/shard_map/ppermute | solution.py:21
where the time goes:
time: 435 us; the launch traced here: 430 us
  local copies, waits for them, and re-layouts  206 us (47%)
  other arithmetic  104 us (24%)
  waiting for transfers between devices  54.8 us (13%)
  matrix products  29.8 us (7%)
  blocking collectives  21.4 us (5%)
  between operations  8.09 us (2%)
  starting transfers between devices  5.85 us (1%)
    gather x1, local copies, waits for them, and re-layouts, pick(): return lax.dynamic_slice_in_dim(rows, start, band_width, rows.ndim - 1)  72.6 us
    transpose x1, local copies, waits for them, and re-layouts, pick(): return lax.dynamic_slice_in_dim(rows, start, band_width, rows.ndim - 1)  68.7 us
    div x1, local copies, waits for them, and re-layouts, local(): return band_rows(both, BAND) / regrouped.shape[1]  57.2 us
    ppermute x5, waiting for transfers between devices, passed_along(): return lax.ppermute(block, axis, route)  54.8 us
    div x1, other arithmetic, local(): return band_rows(both, BAND) / regrouped.shape[1]  43.6 us
    convert_element_type x2, other arithmetic, build_tables(): cosine = (tapering * cos_values).astype(jnp.bfloat16)  31.5 us
    all_to_all x1, blocking collectives, local(): lax.all_to_all(whitened, 'tm', split_axis=0, concat_axis=1, tiled=True)  21.4 us
    dot_general x1, matrix products, local(): jnp.einsum('fwrc,fwsj->frscj', regrouped, extended, preferred_element_typ...  18.4 us
  transfers between devices with their start and end apart: 5, of which 3 were waited for; matrix products, arithmetic and copies ran while one was open for 8% of the time, Pallas kernels for 0%

commit v1 on v0

--- a/solution.py
+++ b/solution.py
@@ -1,8 +1,11 @@
+import functools
 import math
 
 import jax
 import jax.numpy as jnp
 from jax import lax
+from jax.experimental import pallas as pl
+from jax.experimental.pallas import tpu as pltpu
 from jax.sharding import PartitionSpec as P
 
 KEEP = 288
@@ -65,8 +68,8 @@
     scaling = alive_mask.astype(jnp.float32)[None, None, :] / (smoothed + epsilon)
     white_real = real_part[:, HALF : HALF + KEEP] * scaling
     white_imag = imag_part[:, HALF : HALF + KEEP] * scaling
-    whitened = jnp.stack([white_real, white_imag], 2).astype(jnp.bfloat16)
-    return jnp.transpose(whitened, (1, 0, 2, 3))
+    whitened = jnp.concatenate([white_real, white_imag], 0).astype(jnp.bfloat16)
+    return jnp.transpose(whitened, (1, 0, 2))
 
 
 def transform(frames, tables, block_length):
@@ -81,14 +84,56 @@
     return totals
 
 
-def band_rows(gram, band_width):
-    row_count = gram.shape[-2]
+def gram_kernel(piece_count, *refs):
+    pieces = refs[:piece_count]
+    out_ref = refs[piece_count]
+    bins, rows, width = pieces[0].shape
+    band = out_ref.shape[3]
+    window_count = rows // 2
+    row = lax.broadcasted_iota(jnp.int32, (rows, rows), 0)
+    column = lax.broadcasted_iota(jnp.int32, (rows, rows), 1)
+    first_half = row % 8 < 4
+    swap = jnp.where(
+        first_half & (column == row + 4),
+        1.0,
+        jnp.where(~first_half & (column == row - 4), -1.0, 0.0),
+    ).astype(jnp.bfloat16)
+    lane = lax.broadcasted_iota(jnp.int32, (width, width), 0)
+    mirror_lane = lax.broadcasted_iota(jnp.int32, (width, width), 1)
+    mirror = jnp.where(lane + mirror_lane == width - 1, 1.0, 0.0).astype(jnp.bfloat16)
+    upside_down = 7 - lax.broadcasted_iota(jnp.int32, (8, band), 0)
+    contract = (((0,), (0,)), ((), ()))
+    span = piece_count * width
+    for f in range(bins):
+        own = jnp.dot(pieces[0][f], mirror, preferred_element_type=jnp.float32).astype(jnp.bfloat16)
+        rotated = jnp.dot(swap, own, preferred_element_type=jnp.float32).astype(jnp.bfloat16)
+        joined = jnp.concatenate([piece[f] for piece in pieces], 1)
+        if span < band + width:
+            joined = jnp.concatenate(
+                [joined, jnp.zeros((rows, band + width - span), jnp.bfloat16)], 1
+            )
+        for part, left in enumerate((own, rotated)):
+            gram = lax.dot_general(left, joined, contract, preferred_element_type=jnp.float32)
+            skewed = pltpu.roll(gram, band + 1, 1, stride=1, stride_axis=0)
+            for first in range(0, width, 8):
+                rows_of_eight = skewed[width - 8 - first : width - first, :band]
+                out_ref[part, f, first : first + 8] = jnp.take_along_axis(
+                    rows_of_eight, upside_down, axis=0
+                ) * (1.0 / window_count)
 
-    def pick(rows, start):
-        return lax.dynamic_slice_in_dim(rows, start, band_width, rows.ndim - 1)
 
-    starts = lax.iota(jnp.int32, row_count)
-    return jax.vmap(pick, in_axes=(gram.ndim - 2, 0), out_axes=gram.ndim - 2)(gram, starts)
+def stacked_bands(pieces):
+    bins, rows, width = pieces[0].shape
+    block = 2
+    return pl.pallas_call(
+        functools.partial(gram_kernel, len(pieces)),
+        grid=(bins // block,),
+        in_specs=[pl.BlockSpec((block, rows, width), lambda i: (i, 0, 0))] * len(pieces),
+        out_specs=pl.BlockSpec((2, block, width, BAND), lambda i: (0, i, 0, 0)),
+        out_shape=jax.ShapeDtypeStruct((2, bins, width, BAND), jnp.float32),
+        compiler_params=pltpu.CompilerParams(vmem_limit_bytes=48 * 2**20),
+        name="stacked_bands",
+    )(*pieces)
 
 
 def local(record, window_starts, alive_mask):
@@ -110,14 +155,9 @@
     regrouped = lax.all_to_all(whitened, "tm", split_axis=0, concat_axis=1, tiled=True)
     reach_count = BAND // local_width
     pieces = [regrouped]
-    for distance in range(1, reach_count + 1):
+    for distance in range(1, min(reach_count + 1, lax.axis_size("chan"))):
         pieces.append(passed_along(regrouped, "chan", -distance))
-    extended = jnp.concatenate(pieces, 3)
-    blocks = jnp.einsum("fwrc,fwsj->frscj", regrouped, extended, preferred_element_type=jnp.float32)
-    real_gram = blocks[:, 0, 0] + blocks[:, 1, 1]
-    imag_gram = blocks[:, 1, 0] - blocks[:, 0, 1]
-    both = jnp.stack([real_gram, imag_gram], 0)
-    return band_rows(both, BAND) / regrouped.shape[1]
+    return stacked_bands(pieces)
 
 
 def solution(mesh):

time: 435 us -> 162 us (0.37); the launches traced: 430 us -> 162 us
  local copies, waits for them, and re-layouts: 206 us -> 5.62 us
  other arithmetic: 104 us -> 35.4 us
  Pallas kernels: 0 us -> 18.7 us
  matrix products: 29.8 us -> 11.4 us
    gather x1 -> x0, local copies, waits for them, and re-layouts: 72.6 us -> none  [pick(): return lax.dynamic_slice_in_dim(rows, start, band_width, rows.ndim - 1)]
    transpose x2 -> x1, local copies, waits for them, and re-layouts: 69 us -> 0.23 us  [whiten(): return jnp.transpose(whitened, (1, 0, 2))]
    div x1 -> x0, local copies, waits for them, and re-layouts: 57.2 us -> none  [local(): return band_rows(both, BAND) / regrouped.shape[1]]
    div x1 -> x0, other arithmetic: 43.6 us -> none  [local(): return band_rows(both, BAND) / regrouped.shape[1]]
    pallas_call x0 -> x1, Pallas kernels: none -> 18.7 us  [stacked_bands(): pl.pallas_call(functools.partial(gram_kernel, len(pieces)), grid=(bins //...]
    dot_general x1 -> x0, matrix products: 18.4 us -> none  [local(): jnp.einsum('fwrc,fwsj->frscj', regrouped, extended, preferred_element_typ...]
    add x1 -> x0, other arithmetic: 8.48 us -> none  [local(): real_gram = blocks[:, 0, 0] + blocks[:, 1, 1]]
    sub x1 -> x0, other arithmetic: 8.47 us -> none  [local(): imag_gram = blocks[:, 1, 0] - blocks[:, 0, 1]]
  transfers between devices with their start and end apart: 5 -> 4, of which waited for: 3 -> 3; matrix products, arithmetic and copies ran while one was open for 8% -> 21% of each run, Pallas kernels for 0% -> 0%
where the time goes in v1:
time: 162 us
  waiting for transfers between devices  56 us (35%)
  other arithmetic  35.4 us (22%)
  blocking collectives  21.4 us (13%)
  Pallas kernels  18.7 us (12%)
  matrix products  11.4 us (7%)
  between operations  7.99 us (5%)
  local copies, waits for them, and re-layouts  5.62 us (3%)
  starting transfers between devices  5.16 us (3%)
    ppermute x4, waiting for transfers between devices, passed_along(): return lax.ppermute(block, axis, route)  56 us
    convert_element_type x2, other arithmetic, build_tables(): cosine = (tapering * cos_values).astype(jnp.bfloat16)  31.5 us
    all_to_all x1, blocking collectives, local(): lax.all_to_all(whitened, 'tm', split_axis=0, concat_axis=1, tiled=True)  21.4 us
    pallas_call x1, Pallas kernels, stacked_bands(): pl.pallas_call(functools.partial(gram_kernel, len(pieces)), grid=(bins //...  18.7 us
    dot_general x6, matrix products, transform(): jnp.einsum('ft,wtc->wfc', lookup, segment, preferred_element_type=jnp.flo...  10.3 us
    ppermute x4, starting transfers between devices, passed_along(): return lax.ppermute(block, axis, route)  5.16 us
    another operation x1, local copies, waits for them, and re-layouts, local(): jnp.stack([lax.dynamic_slice_in_dim(joined, offsets[number], window_lengt...  3.43 us
  transfers between devices with their start and end apart: 4, of which 3 were waited for; matrix products, arithmetic and copies ran while one was open for 21% of the time, Pallas kernels for 0%

profile of v1, /device:TPU:0, one launch (start us, length us, event | category | flops | bytes accessed | tf_op | source)
XLA Modules:
  0.0 161.6 jit_solution(4000619412864211486)
XLA Ops:
  0.0 1.3 collective-permute-start
  2.0 0.7 broadcast_subtract_fusion
  2.7 0.7 fusion.92
  8.5 0.7 convert_element_type.227
  11.8 12.9 %multiply_convert_fusion.9 = (bf16[352,2048]{1,0:T(8,128)(2,1)S(1)}, bf16[352,2048]{1,0:T(8,128)(2,1)S(1)}) fusion(f32[352]{0:T(512)S(1)} %get-tuple-element.53, f32[352]{0:T(512)S(1)} %get-tuple-element.54, f32[2048]{0:T(1024)S(1)} %get-tuple-element.51, s32[352]{0:T(512)S(1)} %iota_add_fusion.1, f32[2048]{0:T(1024)S(1)} %get-tuple-element.52), kind=kLoop, calls=%fused_computation.41 | loop fusion | flops 13697024 | bytes 2904192 | tf_op jit(solution)/shard_map/convert_element_type | solution.py:47
  24.7 18.6 %multiply_convert_fusion.1 = (bf16[352,2048]{1,0:T(8,128)(2,1)S(1)}, bf16[352,2048]{1,0:T(8,128)(2,1)S(1)}, bf16[352,2048]{1,0:T(8,128)(2,1)}, bf16[352,2048]{1,...) fusion(f32[352]{0:T(512)S(1)} %get-tuple-element.43, ...), kind=kLoop, calls=%fused_computation.33 | loop fusion | flops 41091072 | bytes 14512512 | tf_op jit(solution)/shard_map/convert_element_type | solution.py:47
  43.5 29.6 %collective-permute-done = bf16[12288,128]{1,0:T(8,128)(2,1)S(1)} collective-permute-done((bf16[12288,128]{1,0:T(8,128)(2,1)}, bf16[12288,128]{1,0:T(8,128)(2,1)S(1)}, u32[]{:S(2)}, u32[]{:S(2)}) %collective-permute-start) | collective-permute-done | bytes 3145760 | tf_op jit(solution)/shard_map/ppermute | solution.py:24
  73.1 0.4 constant_dynamic-update-slice_fusion
  73.6 3.4 %dynamic-slice_bitcast_fusion.3 = (bf16[1,12288,128]{2,1,0:T(8,128)(2,1)S(1)}, bf16[1,12288,128]{2,1,0:T(8,128)(2,1)S(1)}, bf16[1,12288,128]{2,1,0:T(8,128)(2,1)S(1)}, bf16[1,12288,128]{2,1,0:T(8,128)(2,1)S(1)}) fusion(bf16[24576,128]{1,0:T(8,128)(2,1)S(1)} %constant_dynamic-update-slice_fusion, s32[]{:T(128)S(6)} %select_n.114, s32[]{:T(128)S(6)} %select_n.117, ...), kind=kLoop, calls=%fused_computation.5 | loop fusion | bytes 25165840 | tf_op jit(solution)/shard_map/stack | solution.py:147
  77.0 1.8 %pad_maximum_fusion = bf16[4,12288,128]{2,1,0:T(8,128)(2,1)S(1)} fusion(bf16[1,12288,128]{2,1,0:T(8,128)(2,1)S(1)} %get-tuple-element.6, bf16[1,12288,128]{2,1,0:T(8,128)(2,1)S(1)} %get-tuple-element.7, bf16[1,12288,128]{2,1,0:T(8,128)(2,1)S(1)} %get-tuple-element.8, bf16[1,12288,128]{2,1,0:T(8,128)(2,1)S(1)} %get-tuple-element.5), kind=kLoop, calls=%fused_computation | loop fusion | flops 18874368 | bytes 25165824 | tf_op jit(solution)/shard_map/stack | solution.py:147
  78.9 1.7 %fusion.5 = f32[4,128,704]{1,2,0:T(8,128)S(1)} fusion(bf16[352,2048]{1,0:T(8,128)(2,1)S(1)} %get-tuple-element.14, bf16[352,2048]{1,0:T(8,128)(2,1)S(1)} %get-tuple-element.13, bf16[4,12288,128]{2,1,0:T(8,128)(2,1)S(1)} %pad_maximum_fusion), kind=kOutput, calls=%fused_computation.13 | convolution fusion | flops 1482162176 | bytes 6422528 | tf_op jit(solution)/shard_map/ft,wtc->wfc/dot_general | solution.py:81
  80.7 1.7 %fusion.2 = f32[4,128,704]{1,2,0:T(8,128)S(1)} fusion(bf16[352,2048]{1,0:T(8,128)(2,1)S(1)} %copy-done.7, bf16[352,2048]{1,0:T(8,128)(2,1)S(1)} %copy-done.8, bf16[4,12288,128]{2,1,0:T(8,128)(2,1)S(1)} %pad_maximum_fusion), kind=kOutput, calls=%fused_computation.9 | convolution fusion | flops 1482162176 | bytes 6422528 | tf_op jit(solution)/shard_map/ft,wtc->wfc/dot_general | solution.py:81
  82.5 1.7 %fusion.8 = f32[4,128,704]{1,2,0:T(8,128)S(1)} fusion(bf16[352,2048]{1,0:T(8,128)(2,1)S(1)} %copy-done.5, bf16[352,2048]{1,0:T(8,128)(2,1)S(1)} %copy-done.6, bf16[4,12288,128]{2,1,0:T(8,128)(2,1)S(1)} %pad_maximum_fusion), kind=kOutput, calls=%fused_computation.17 | convolution fusion | flops 1482162176 | bytes 6422528 | tf_op jit(solution)/shard_map/ft,wtc->wfc/dot_general | solution.py:81
  84.3 1.7 %fusion.11 = f32[4,128,704]{1,2,0:T(8,128)S(1)} fusion(bf16[352,2048]{1,0:T(8,128)(2,1)S(1)} %copy-done.3, bf16[352,2048]{1,0:T(8,128)(2,1)S(1)} %copy-done.4, bf16[4,12288,128]{2,1,0:T(8,128)(2,1)S(1)} %pad_maximum_fusion), kind=kOutput, calls=%fused_computation.21 | convolution fusion | flops 1482162176 | bytes 6422528 | tf_op jit(solution)/shard_map/ft,wtc->wfc/dot_general | solution.py:81
  86.1 1.7 %fusion.14 = f32[4,128,704]{1,2,0:T(8,128)S(1)} fusion(bf16[352,2048]{1,0:T(8,128)(2,1)S(1)} %copy-done.1, bf16[352,2048]{1,0:T(8,128)(2,1)S(1)} %copy-done.2, bf16[4,12288,128]{2,1,0:T(8,128)(2,1)S(1)} %pad_maximum_fusion), kind=kOutput, calls=%fused_computation.25 | convolution fusion | flops 1482162176 | bytes 6422528 | tf_op jit(solution)/shard_map/ft,wtc->wfc/dot_general | solution.py:81
  87.7 2.0 %add_bitcast_fusion = f32[4,704,128]{2,1,0:T(8,128)S(1)} fusion(f32[4,128,704]{1,2,0:T(8,128)S(1)} %fusion.14, f32[4,128,704]{1,2,0:T(8,128)S(1)} %fusion.11, f32[4,128,704]{1,2,0:T(8,128)S(1)} %fusion.8, f32[4,128,704]{1,2,0:T(8,128)S(1)} %fusion.2, f32[4,128,704]{1,2,0:T(8,128)S(1)} %fusion.5, bf16[4,12288,128]{2,1,0:T(8,128)(2,1)S(1)} %pad_maximum_fusion, ...), kind=kOutput, calls=%fused_computation.56 | convolution fusion | flops 1483964416 | bytes 13631488 | tf_op jit(solution)/shard_map/ft,wtc->wfc/dot_general | solution.py:81
  89.7 1.1 fusion.40
  91.1 21.4 %all_to_all.18 = bf16[288,8,128]{2,1,0:T(8,128)(2,1)S(1)} all-to-all(bf16[288,8,128]{2,1,0:T(8,128)(2,1)S(1)} %copy.7), channel_id=1, replica_groups=mesh['tm'=8,'chan'=4] {'tm'}, dimensions={0} | all-to-all | bytes 1179648 | tf_op jit(solution)/shard_map/all_to_all | solution.py:155
  112.7 1.3 collective-permute-start.1
  114.0 1.3 collective-permute-start.2
  115.3 1.3 collective-permute-start.3
  116.6 24.3 %collective-permute-done.2.refs_2_ = bf16[36,64,128]{2,1,0:T(8,128)(2,1)S(1)} collective-permute-done((bf16[36,64,128]{2,1,0:T(8,128)(2,1)S(1)}, bf16[36,64,128]{2,1,0:T(8,128)(2,1)S(1)}, u32[]{:S(2)}, u32[]{:S(2)}) %collective-permute-start.2) | collective-permute-done | bytes 589856 | tf_op jit(solution)/shard_map/ppermute | solution.py:24
  140.9 2.0 %collective-permute-done.3.refs_3_ = bf16[36,64,128]{2,1,0:T(8,128)(2,1)S(1)} collective-permute-done((bf16[36,64,128]{2,1,0:T(8,128)(2,1)S(1)}, bf16[36,64,128]{2,1,0:T(8,128)(2,1)S(1)}, u32[]{:S(2)}, u32[]{:S(2)}) %collective-permute-start.3) | collective-permute-done | bytes 589856 | tf_op jit(solution)/shard_map/ppermute | solution.py:24
  142.9 18.7 %stacked_bands.1 = f32[2,36,128,512]{3,2,1,0:T(8,128)} custom-call(bf16[36,64,128]{2,1,0:T(8,128)(2,1)S(1)} %bitcast.52, bf16[36,64,128]{2,1,0:T(8,128)(2,1)S(1)} %collective-permute-done.1.refs_1_, bf16[36,64,128]{2,1,0:T(8,128)(2,1)S(1)} %collective-permute-done.2.refs_2_, bf16[36,64,128]{2,1,0:T(8,128)(2,1)S(1)} %collective-permute-done.3.refs_3_), custom_call_target="tpu_custom_call" | custom-call | tf_op jit(solution)/shard_map/stacked_bands/pallas_call | solution.py:128
  (36 shorter events, 1.8 us)
Async XLA Ops:
  0.0 73.1 %collective-permute-start = (bf16[12288,128]{1,0:T(8,128)(2,1)}, bf16[12288,128]{1,0:T(8,128)(2,1)S(1)}, u32[]{:S(2)}, u32[]{:S(2)}) collective-permute-start(bf16[12288,128]{1,0:T(8,128)(2,1)} %param.3), channel_id=1, source_target_pairs={{4,0},{8,4},{12,8},{16,12},{20,16},{24,20},{28,24},{5,1},{9,5},{13... | collective-permute-start | bytes 9437192 | tf_op jit(solution)/shard_map/ppermute | solution.py:24
  24.7 18.6 %copy-start = (bf16[12288,128]{1,0:T(8,128)(2,1)S(1)}, bf16[12288,128]{1,0:T(8,128)(2,1)}, u32[]{:S(2)}) copy-start(bf16[12288,128]{1,0:T(8,128)(2,1)} %param.3) | copy-start | bytes 9437188
  78.9 1.7 %copy-start.7 = (bf16[352,2048]{1,0:T(8,128)(2,1)S(1)}, bf16[352,2048]{1,0:T(8,128)(2,1)}, u32[]{:S(2)}) copy-start(bf16[352,2048]{1,0:T(8,128)(2,1)} %get-tuple-element.27) | copy-start | bytes 4325380
  78.9 1.8 %copy-start.8 = (bf16[352,2048]{1,0:T(8,128)(2,1)S(1)}, bf16[352,2048]{1,0:T(8,128)(2,1)}, u32[]{:S(2)}) copy-start(bf16[352,2048]{1,0:T(8,128)(2,1)} %get-tuple-element.28) | copy-start | bytes 4325380
  80.7 1.7 %copy-start.5 = (bf16[352,2048]{1,0:T(8,128)(2,1)S(1)}, bf16[352,2048]{1,0:T(8,128)(2,1)}, u32[]{:S(2)}) copy-start(bf16[352,2048]{1,0:T(8,128)(2,1)} %get-tuple-element.25) | copy-start | bytes 4325380
  80.7 1.8 %copy-start.6 = (bf16[352,2048]{1,0:T(8,128)(2,1)S(1)}, bf16[352,2048]{1,0:T(8,128)(2,1)}, u32[]{:S(2)}) copy-start(bf16[352,2048]{1,0:T(8,128)(2,1)} %get-tuple-element.26) | copy-start | bytes 4325380
  82.5 1.7 %copy-start.3 = (bf16[352,2048]{1,0:T(8,128)(2,1)S(1)}, bf16[352,2048]{1,0:T(8,128)(2,1)}, u32[]{:S(2)}) copy-start(bf16[352,2048]{1,0:T(8,128)(2,1)} %get-tuple-element.23) | copy-start | bytes 4325380
  82.5 1.8 %copy-start.4 = (bf16[352,2048]{1,0:T(8,128)(2,1)S(1)}, bf16[352,2048]{1,0:T(8,128)(2,1)}, u32[]{:S(2)}) copy-start(bf16[352,2048]{1,0:T(8,128)(2,1)} %get-tuple-element.24) | copy-start | bytes 4325380
  84.3 1.7 %copy-start.1 = (bf16[352,2048]{1,0:T(8,128)(2,1)S(1)}, bf16[352,2048]{1,0:T(8,128)(2,1)}, u32[]{:S(2)}) copy-start(bf16[352,2048]{1,0:T(8,128)(2,1)} %get-tuple-element.21) | copy-start | bytes 4325380
  84.3 1.8 %copy-start.2 = (bf16[352,2048]{1,0:T(8,128)(2,1)S(1)}, bf16[352,2048]{1,0:T(8,128)(2,1)}, u32[]{:S(2)}) copy-start(bf16[352,2048]{1,0:T(8,128)(2,1)} %get-tuple-element.22) | copy-start | bytes 4325380
  112.7 3.9 %collective-permute-start.1 = (bf16[36,64,128]{2,1,0:T(8,128)(2,1)S(1)}, bf16[36,64,128]{2,1,0:T(8,128)(2,1)S(1)}, u32[]{:S(2)}, u32[]{:S(2)}) collective-permute-start(bf16[36,64,128]{2,1,0:T(8,128)(2,1)S(1)} %bitcast.49), channel_id=1, source_target_pairs={{1,0},{2,1},{3,2},{5,4},{6,5},{7,6},{9,8},{10,9},{11,10},{13,12},{... | collective-permute-start | bytes 1769480 | tf_op jit(solution)/shard_map/ppermute | solution.py:24
  114.0 26.9 %collective-permute-start.2 = (bf16[36,64,128]{2,1,0:T(8,128)(2,1)S(1)}, bf16[36,64,128]{2,1,0:T(8,128)(2,1)S(1)}, u32[]{:S(2)}, u32[]{:S(2)}) collective-permute-start(bf16[36,64,128]{2,1,0:T(8,128)(2,1)S(1)} %bitcast.50), channel_id=1, source_target_pairs={{2,0},{3,1},{6,4},{7,5},{10,8},{11,9},{14,12},{15,13},{18,16},{19,... | collective-permute-start | bytes 1769480 | tf_op jit(solution)/shard_map/ppermute | solution.py:24
  115.3 27.6 %collective-permute-start.3 = (bf16[36,64,128]{2,1,0:T(8,128)(2,1)S(1)}, bf16[36,64,128]{2,1,0:T(8,128)(2,1)S(1)}, u32[]{:S(2)}, u32[]{:S(2)}) collective-permute-start(bf16[36,64,128]{2,1,0:T(8,128)(2,1)S(1)} %bitcast.51), channel_id=1, source_target_pairs={{3,0},{7,4},{11,8},{15,12},{19,16},{23,20},{27,24},{31,28}} | collective-permute-start | bytes 1769480 | tf_op jit(solution)/shard_map/ppermute | solution.py:24

commit v2 on v1

--- a/solution.py
+++ b/solution.py
@@ -3,6 +3,7 @@
 
 import jax
 import jax.numpy as jnp
+import numpy as np
 from jax import lax
 from jax.experimental import pallas as pl
 from jax.experimental.pallas import tpu as pltpu
@@ -24,30 +25,71 @@
     return lax.ppermute(block, axis, route)
 
 
-def build_tables(window_length):
+def base_tables(window_length, block_length):
+    step_angle = 2.0 * np.pi / window_length
+    bin_numbers = FLO - HALF + np.arange(KEEP + 2 * HALF)
+    times = np.arange(block_length)
+    firsts = np.arange(0, window_length, block_length)
+    base = step_angle * (bin_numbers[:, None] * times[None, :] % window_length)
+    shift = step_angle * (bin_numbers[None, :, None] * firsts[:, None, None] % window_length)
+    tapering = 0.5 - 0.5 * np.cos(step_angle * (firsts[:, None, None] + times[None, None, :]))
+    values = (np.cos(base), np.sin(base), np.cos(shift), np.sin(shift), tapering)
+    return [value.astype(np.float32) for value in values]
+
+
+def dft_kernel(cos_ref, sin_ref, shift_cos_ref, shift_sin_ref, taper_ref, frames_ref, out_ref):
+    bin_count, block_length = cos_ref.shape
+    shift_cos = shift_cos_ref[0]
+    shift_sin = shift_sin_ref[0]
+
+    @pl.when(pl.program_id(0) == 0)
+    def _():
+        out_ref[...] = jnp.zeros_like(out_ref)
+
+    pieces = []
+    for first in range(0, block_length, 256):
+        span = slice(first, first + 256)
+        base_cos = cos_ref[:, span]
+        base_sin = sin_ref[:, span]
+        tapering = taper_ref[0, :, span]
+        cosine = tapering * (base_cos * shift_cos - base_sin * shift_sin)
+        sine = -tapering * (base_sin * shift_cos + base_cos * shift_sin)
+        pieces.append(jnp.concatenate([cosine, sine], 0).astype(jnp.bfloat16))
+    lookup = jnp.concatenate(pieces, 1)
+    width = frames_ref.shape[2]
+    for number in range(0, WPD, 2):
+        pair = jnp.concatenate([frames_ref[number], frames_ref[number + 1]], 1)
+        out_ref[:, number * width : (number + 2) * width] += jnp.dot(
+            lookup, pair, preferred_element_type=jnp.float32
+        )
+
+
+def transform(frames):
+    count, window_length, width = frames.shape
+    block_length = math.gcd(window_length, 1024)
     bin_count = KEEP + 2 * HALF
-    block_length = math.gcd(window_length, 2048)
-    step_angle = 2.0 * math.pi / window_length
-    bin_numbers = FLO - HALF + lax.iota(jnp.int32, bin_count)
-    base_times = lax.iota(jnp.int32, block_length)
-    base_phases = bin_numbers[:, None] * base_times[None, :] % window_length
-    base_angles = step_angle * base_phases.astype(jnp.float32)
-    base_cos = jnp.cos(base_angles)
-    base_sin = jnp.sin(base_angles)
-    tables = []
-    for first_time in range(0, window_length, block_length):
-        shift_phases = bin_numbers * first_time % window_length
-        shift_angles = step_angle * shift_phases.astype(jnp.float32)
-        shift_cos = jnp.cos(shift_angles)[:, None]
-        shift_sin = jnp.sin(shift_angles)[:, None]
-        sample_times = (first_time + base_times).astype(jnp.float32)
-        tapering = (0.5 - 0.5 * jnp.cos(step_angle * sample_times))[None, :]
-        cos_values = base_cos * shift_cos - base_sin * shift_sin
-        sin_values = base_sin * shift_cos + base_cos * shift_sin
-        cosine = (tapering * cos_values).astype(jnp.bfloat16)
-        sine_rows = (-tapering * sin_values).astype(jnp.bfloat16)
-        tables.append(jnp.concatenate([cosine, sine_rows], 0))
-    return (tables, block_length)
+    steps = window_length // block_length
+    return pl.pallas_call(
+        dft_kernel,
+        grid=(steps,),
+        in_specs=[
+            pl.BlockSpec((bin_count, block_length), lambda i: (0, 0)),
+            pl.BlockSpec((bin_count, block_length), lambda i: (0, 0)),
+            pl.BlockSpec((1, bin_count, 1), lambda i: (i, 0, 0)),
+            pl.BlockSpec((1, bin_count, 1), lambda i: (i, 0, 0)),
+            pl.BlockSpec((1, 1, block_length), lambda i: (i, 0, 0)),
+            pl.BlockSpec((count, block_length, width), lambda i: (0, i, 0)),
+        ],
+        out_specs=pl.BlockSpec((2 * bin_count, count * width), lambda i: (0, 0)),
+        out_shape=jax.ShapeDtypeStruct((2 * bin_count, count * width), jnp.float32),
+        compiler_params=pltpu.CompilerParams(vmem_limit_bytes=40 * 2**20),
+        cost_estimate=pl.CostEstimate(
+            flops=4 * bin_count * count * width * window_length,
+            bytes_accessed=2 * count * width * window_length,
+            transcendentals=0,
+        ),
+        name="windowed_transform",
+    )(*base_tables(window_length, block_length), frames)
 
 
 def smoother_matrix():
@@ -59,29 +101,17 @@
 
 def whiten(spectra, alive_mask):
     bin_count = KEEP + 2 * HALF
-    real_part = spectra[:, :bin_count]
-    imag_part = spectra[:, bin_count:]
+    width = alive_mask.shape[0]
+    real_part = spectra[:bin_count]
+    imag_part = spectra[bin_count:]
     magnitude = jnp.sqrt(real_part * real_part + imag_part * imag_part)
-    smoothed = jnp.einsum(
-        "kj,wjc->wkc", smoother_matrix(), magnitude, precision=lax.Precision.HIGHEST
-    ) / (2 * HALF + 1)
-    scaling = alive_mask.astype(jnp.float32)[None, None, :] / (smoothed + epsilon)
-    white_real = real_part[:, HALF : HALF + KEEP] * scaling
-    white_imag = imag_part[:, HALF : HALF + KEEP] * scaling
-    whitened = jnp.concatenate([white_real, white_imag], 0).astype(jnp.bfloat16)
-    return jnp.transpose(whitened, (1, 0, 2))
-
-
-def transform(frames, tables, block_length):
-    bin_count = KEEP + 2 * HALF
-    totals = jnp.zeros((frames.shape[0], 2 * bin_count, frames.shape[2]), jnp.float32)
-    for number, lookup in enumerate(tables):
-        first_time = number * block_length
-        segment = frames[:, first_time : first_time + block_length]
-        totals = totals + jnp.einsum(
-            "ft,wtc->wfc", lookup, segment, preferred_element_type=jnp.float32
-        )
-    return totals
+    smoothed = jnp.dot(smoother_matrix(), magnitude, precision=lax.Precision.HIGHEST)
+    smoothed = smoothed / (2 * HALF + 1)
+    scaling = jnp.tile(alive_mask.astype(jnp.float32), WPD)[None, :] / (smoothed + epsilon)
+    white_real = real_part[HALF : HALF + KEEP] * scaling
+    white_imag = imag_part[HALF : HALF + KEEP] * scaling
+    whitened = jnp.concatenate([white_real, white_imag], 1).astype(jnp.bfloat16)
+    return whitened.reshape(KEEP, 2 * WPD, width)
 
 
 def gram_kernel(piece_count, *refs):
@@ -136,21 +166,27 @@
     )(*pieces)
 
 
-def local(record, window_starts, alive_mask):
-    window_length = record.shape[0]
-    local_width = record.shape[1]
-    tables, block_length = build_tables(window_length)
-    index_time = lax.axis_index("tm")
-    offsets = window_starts - index_time * window_length
-    following = passed_along(record, "tm", -1)
-    joined = jnp.concatenate([record, following], 0)
-    frames = jnp.stack(
+def cut(joined, offsets, window_length):
+    return jnp.stack(
         [
             lax.dynamic_slice_in_dim(joined, offsets[number], window_length, 0)
             for number in range(WPD)
         ]
     )
-    spectra = transform(frames, tables, block_length)
+
+
+def local(record, window_starts, alive_mask):
+    window_length = record.shape[0]
+    local_width = record.shape[1]
+    index_time = lax.axis_index("tm")
+    offsets = window_starts - index_time * window_length
+    earlier_offsets = passed_along(offsets, "tm", 1)
+    silence = jnp.zeros_like(record)
+    tails = cut(jnp.concatenate([silence, record], 0), earlier_offsets, window_length)
+    tail_spectra = transform(tails)
+    following = passed_along(tail_spectra, "tm", -1)
+    heads = cut(jnp.concatenate([record, silence], 0), offsets, window_length)
+    spectra = transform(heads) + following
     whitened = whiten(spectra, alive_mask)
     regrouped = lax.all_to_all(whitened, "tm", split_axis=0, concat_axis=1, tiled=True)
     reach_count = BAND // local_width

time: 162 us -> 172 us (1.062)
  Pallas kernels: 18.7 us -> 48.7 us
  other arithmetic: 35.4 us -> 18.2 us
  waiting for transfers between devices: 56 us -> 41 us
  local copies, waits for them, and re-layouts: 5.62 us -> 16.5 us
  matrix products: 11.4 us -> 1.03 us
  between operations: 7.99 us -> 14.9 us
  starting transfers between devices: 5.16 us -> 10 us
    convert_element_type x3 -> x1, other arithmetic: 32.2 us -> 0.66 us  [whiten(): alive_mask.astype(jnp.float32)]
    pallas_call x0 -> x2, Pallas kernels: none -> 30.1 us  [transform(): pl.pallas_call(dft_kernel, grid=(steps,), in_specs=[pl.BlockSpec((bin_cou...]
    ppermute x4 -> x5, waiting for transfers between devices: 56 us -> 41 us  [passed_along(): return lax.ppermute(block, axis, route)]
    another operation x1 -> x2, other arithmetic: 1.85 us -> 16.2 us  [cut(): jnp.stack([lax.dynamic_slice_in_dim(joined, offsets[number], window_lengt...]
    another operation x1, local copies, waits for them, and re-layouts: 3.43 us -> 14.9 us  [cut(): jnp.stack([lax.dynamic_slice_in_dim(joined, offsets[number], window_lengt...]
    dot_general x7 -> x1, matrix products: 11.4 us -> 1.03 us  [whiten(): jnp.dot(smoother_matrix(), magnitude, precision=lax.Precision.HIGHEST)]
    ppermute x4 -> x5, starting transfers between devices: 5.16 us -> 10 us  [passed_along(): return lax.ppermute(block, axis, route)]
  transfers between devices with their start and end apart: 4 -> 5, of which waited for: 3 -> 3; matrix products, arithmetic and copies ran while one was open for 21% -> 4% of each run, Pallas kernels for 0% -> 9%
where the time goes in v2:
time: 172 us; the launch traced here: 171 us
  Pallas kernels  48.7 us (28%)
  waiting for transfers between devices  41 us (24%)
  blocking collectives  20.2 us (12%)
  other arithmetic  18.2 us (11%)
  local copies, waits for them, and re-layouts  16.5 us (10%)
  between operations  14.9 us (9%)
  starting transfers between devices  10 us (6%)
    ppermute x5, waiting for transfers between devices, passed_along(): return lax.ppermute(block, axis, route)  41 us
    pallas_call x2, Pallas kernels, transform(): pl.pallas_call(dft_kernel, grid=(steps,), in_specs=[pl.BlockSpec((bin_cou...  30.1 us
    all_to_all x1, blocking collectives, local(): lax.all_to_all(whitened, 'tm', split_axis=0, concat_axis=1, tiled=True)  20.2 us
    pallas_call x1, Pallas kernels, stacked_bands(): pl.pallas_call(functools.partial(gram_kernel, len(pieces)), grid=(bins //...  18.6 us
    another operation x2, other arithmetic, cut(): jnp.stack([lax.dynamic_slice_in_dim(joined, offsets[number], window_lengt...  16.2 us
    another operation x1, local copies, waits for them, and re-layouts, cut(): jnp.stack([lax.dynamic_slice_in_dim(joined, offsets[number], window_lengt...  14.9 us
    ppermute x5, starting transfers between devices, passed_along(): return lax.ppermute(block, axis, route)  10 us
  transfers between devices with their start and end apart: 5, of which 3 were waited for; matrix products, arithmetic and copies ran while one was open for 4% of the time, Pallas kernels for 9%

profile of v2, /device:TPU:0, one launch (start us, length us, event | category | flops | bytes accessed | tf_op | source)
XLA Modules:
  0.0 170.5 jit_solution(15273537919514742508)
XLA Ops:
  0.0 0.7 broadcast_subtract_fusion
  0.7 4.8 %collective-permute-start = (s32[4]{0:T(128)S(1)}, s32[4]{0:T(128)S(1)}, u32[]{:S(2)}, u32[]{:S(2)}) collective-permute-start(s32[4]{0:T(128)S(1)} %broadcast_subtract_fusion), channel_id=1, source_target_pairs={{0,4},{4,8},{8,12},{12,16},{16,20},{20,24},{24,28},{1,5},{5,9},{9,... | collective-permute-start | bytes 56 | tf_op jit(solution)/shard_map/ppermute | solution.py:25
  5.5 0.6 fusion.19
  11.1 0.7 convert_element_type.6
  14.2 0.6 fusion.18
  22.2 14.9 %fusion.4 = (bf16[1,12288,128]{2,1,0:T(8,128)(2,1)S(1)}, bf16[1,12288,128]{2,1,0:T(8,128)(2,1)S(1)}, bf16[1,12288,128]{2,1,0:T(8,128)(2,1)S(1)}, bf16[1,12288,12...) fusion(s32[]{:T(128)S(6)} %select_n.28, ...), kind=kLoop, calls=%fused_computation.14 | loop fusion | bytes 28311584 | tf_op jit(solution)/shard_map/stack | solution.py:170
  37.2 10.8 %pad_maximum_fusion.1.frames_ref = bf16[4,12288,128]{2,1,0:T(8,128)(2,1)} fusion(bf16[1,12288,128]{2,1,0:T(8,128)(2,1)} %get-tuple-element.11, bf16[1,12288,128]{2,1,0:T(8,128)(2,1)} %get-tuple-element.10, bf16[1,12288,128]{2,1,0:T(8,128)(2,1)} %get-tuple-element.9, bf16[1,12288,128]{2,1,0:T(8,128)(2,1)S(1)} %get-tuple-element.5), kind=kLoop, calls=%fused_computation.1 | loop fusion | flops 18874368 | bytes 25165824 | tf_op jit(solution)/shard_map/stack | solution.py:170
  48.0 15.1 %windowed_transform.3 = f32[704,512]{1,0:T(8,128)S(1)} custom-call(f32[352,1024]{1,0:T(8,128)S(1)} %copy-done.2, f32[352,1024]{1,0:T(8,128)S(1)} %copy-done.3, f32[12,352,1]{2,1,0:T(8,128)S(1)} %copy-done, f32[12,352,1]{2,1,0:T(8,128)S(1)} %copy-done.1, f32[12,1,1024]{2,1,0:T(1,128)S(1)} %copy-done.4, bf16[4,12288,128]{2,1,0:T(8,128)(2,1)} %pad_maximum_fusion.1.frames_ref), custom_call_target="tpu_custom_call" | custom-call | flops 8858370048 | bytes 12582912 | tf_op jit(solution)/shard_map/windowed_transform/pallas_call | solution.py:72
  63.0 1.3 collective-permute-start.1
  64.3 5.5 %pad_maximum_fusion.frames_ref = bf16[4,12288,128]{2,1,0:T(8,128)(2,1)} fusion(bf16[1,12288,128]{2,1,0:T(8,128)(2,1)S(1)} %get-tuple-element.8, bf16[1,12288,128]{2,1,0:T(8,128)(2,1)S(1)} %get-tuple-element.7, bf16[1,12288,128]{2,1,0:T(8,128)(2,1)S(1)} %get-tuple-element.6, bf16[1,12288,128]{2,1,0:T(8,128)(2,1)S(1)} %get-tuple-element.12), kind=kLoop, calls=%fused_computation | loop fusion | flops 18874368 | bytes 25165824 | tf_op jit(solution)/shard_map/stack | solution.py:170
  69.8 15.1 %windowed_transform.2 = f32[704,512]{1,0:T(8,128)S(1)} custom-call(f32[352,1024]{1,0:T(8,128)S(1)} %copy-done.2, f32[352,1024]{1,0:T(8,128)S(1)} %copy-done.3, f32[12,352,1]{2,1,0:T(8,128)S(1)} %copy-done, f32[12,352,1]{2,1,0:T(8,128)S(1)} %copy-done.1, f32[12,1,1024]{2,1,0:T(1,128)S(1)} %copy-done.4, bf16[4,12288,128]{2,1,0:T(8,128)(2,1)} %pad_maximum_fusion.frames_ref), custom_call_target="tpu_custom_call" | custom-call | flops 8858370048 | bytes 12582912 | tf_op jit(solution)/shard_map/windowed_transform/pallas_call | solution.py:72
  84.9 14.6 %collective-permute-done.1 = f32[704,512]{1,0:T(8,128)S(1)} collective-permute-done((f32[704,512]{1,0:T(8,128)S(1)}, f32[704,512]{1,0:T(8,128)S(1)}, u32[]{:S(2)}, u32[]{:S(2)}) %collective-permute-start.1) | collective-permute-done | bytes 1441824 | tf_op jit(solution)/shard_map/ppermute | solution.py:25
  99.5 0.3 add.59
  99.8 1.0 fusion.14
  100.8 0.1 concatenate.17
  101.0 0.3 pad_maximum_fusion.2
  101.3 20.2 %all_to_all.18 = bf16[288,8,128]{2,1,0:T(8,128)(2,1)S(1)} all-to-all(bf16[288,8,128]{2,1,0:T(8,128)(2,1)S(1)} %pad_maximum_fusion.2), channel_id=1, replica_groups=mesh['tm'=8,'chan'=4] {'tm'}, dimensions={0} | all-to-all | bytes 1179648 | tf_op jit(solution)/shard_map/all_to_all | solution.py:191
  121.5 0.2 copy.16
  121.6 1.3 collective-permute-start.2
  122.9 1.3 collective-permute-start.3
  124.2 1.3 collective-permute-start.4
  125.6 24.3 %collective-permute-done.3.refs_2_ = bf16[36,64,128]{2,1,0:T(8,128)(2,1)S(1)} collective-permute-done((bf16[36,64,128]{2,1,0:T(8,128)(2,1)S(1)}, bf16[36,64,128]{2,1,0:T(8,128)(2,1)S(1)}, u32[]{:S(2)}, u32[]{:S(2)}) %collective-permute-start.3) | collective-permute-done | bytes 589856 | tf_op jit(solution)/shard_map/ppermute | solution.py:25
  149.9 2.0 %collective-permute-done.4.refs_3_ = bf16[36,64,128]{2,1,0:T(8,128)(2,1)S(1)} collective-permute-done((bf16[36,64,128]{2,1,0:T(8,128)(2,1)S(1)}, bf16[36,64,128]{2,1,0:T(8,128)(2,1)S(1)}, u32[]{:S(2)}, u32[]{:S(2)}) %collective-permute-start.4) | collective-permute-done | bytes 589856 | tf_op jit(solution)/shard_map/ppermute | solution.py:25
  151.9 18.6 %stacked_bands.1 = f32[2,36,128,512]{3,2,1,0:T(8,128)} custom-call(bf16[36,64,128]{2,1,0:T(8,128)(2,1)S(1)} %bitcast.35, bf16[36,64,128]{2,1,0:T(8,128)(2,1)S(1)} %collective-permute-done.2.refs_1_, bf16[36,64,128]{2,1,0:T(8,128)(2,1)S(1)} %collective-permute-done.3.refs_2_, bf16[36,64,128]{2,1,0:T(8,128)(2,1)S(1)} %collective-permute-done.4.refs_3_), custom_call_target="tpu_custom_call" | custom-call | tf_op jit(solution)/shard_map/stacked_bands/pallas_call | solution.py:158
  (15 shorter events, 0.1 us)
Async XLA Ops:
  0.7 13.6 %collective-permute-start = (s32[4]{0:T(128)S(1)}, s32[4]{0:T(128)S(1)}, u32[]{:S(2)}, u32[]{:S(2)}) collective-permute-start(s32[4]{0:T(128)S(1)} %broadcast_subtract_fusion), channel_id=1, source_target_pairs={{0,4},{4,8},{8,12},{12,16},{16,20},{20,24},{24,28},{1,5},{5,9},{9,... | collective-permute-start | bytes 56 | tf_op jit(solution)/shard_map/ppermute | solution.py:25
  37.1 10.8 %copy-start = (f32[12,352,1]{2,1,0:T(8,128)S(1)}, f32[12,352,1]{2,1,0:T(8,128)}, u32[]{:S(2)}) copy-start(f32[12,352,1]{2,1,0:T(8,128)} %constant.33.clone.shift_cos_ref) | copy-start | bytes 50692
  37.1 10.8 %copy-start.1 = (f32[12,352,1]{2,1,0:T(8,128)S(1)}, f32[12,352,1]{2,1,0:T(8,128)}, u32[]{:S(2)}) copy-start(f32[12,352,1]{2,1,0:T(8,128)} %constant.34.clone.shift_sin_ref) | copy-start | bytes 50692
  37.1 10.8 %copy-start.2 = (f32[352,1024]{1,0:T(8,128)S(1)}, f32[352,1024]{1,0:T(8,128)}, u32[]{:S(2)}) copy-start(f32[352,1024]{1,0:T(8,128)} %constant.31.clone.cos_ref) | copy-start | bytes 4325380
  37.1 10.8 %copy-start.3 = (f32[352,1024]{1,0:T(8,128)S(1)}, f32[352,1024]{1,0:T(8,128)}, u32[]{:S(2)}) copy-start(f32[352,1024]{1,0:T(8,128)} %constant.32.clone.sin_ref) | copy-start | bytes 4325380
  37.2 10.8 %copy-start.4 = (f32[12,1,1024]{2,1,0:T(1,128)S(1)}, f32[12,1,1024]{2,1,0:T(1,128)}, u32[]{:S(2)}) copy-start(f32[12,1,1024]{2,1,0:T(1,128)} %constant.35.clone.taper_ref) | copy-start | bytes 147460
  63.0 36.4 %collective-permute-start.1 = (f32[704,512]{1,0:T(8,128)S(1)}, f32[704,512]{1,0:T(8,128)S(1)}, u32[]{:S(2)}, u32[]{:S(2)}) collective-permute-start(f32[704,512]{1,0:T(8,128)S(1)} %windowed_transform.3), channel_id=1, source_target_pairs={{4,0},{8,4},{12,8},{16,12},{20,16},{24,20},{28,24},{5,1},{9,5},{13... | collective-permute-start | bytes 4325384 | tf_op jit(solution)/shard_map/ppermute | solution.py:25
  121.6 3.9 %collective-permute-start.2 = (bf16[36,64,128]{2,1,0:T(8,128)(2,1)S(1)}, bf16[36,64,128]{2,1,0:T(8,128)(2,1)S(1)}, u32[]{:S(2)}, u32[]{:S(2)}) collective-permute-start(bf16[36,64,128]{2,1,0:T(8,128)(2,1)S(1)} %bitcast.32), channel_id=1, source_target_pairs={{1,0},{2,1},{3,2},{5,4},{6,5},{7,6},{9,8},{10,9},{11,10},{13,12},{... | collective-permute-start | bytes 1769480 | tf_op jit(solution)/shard_map/ppermute | solution.py:25
  122.9 26.9 %collective-permute-start.3 = (bf16[36,64,128]{2,1,0:T(8,128)(2,1)S(1)}, bf16[36,64,128]{2,1,0:T(8,128)(2,1)S(1)}, u32[]{:S(2)}, u32[]{:S(2)}) collective-permute-start(bf16[36,64,128]{2,1,0:T(8,128)(2,1)S(1)} %bitcast.33), channel_id=1, source_target_pairs={{2,0},{3,1},{6,4},{7,5},{10,8},{11,9},{14,12},{15,13},{18,16},{19,... | collective-permute-start | bytes 1769480 | tf_op jit(solution)/shard_map/ppermute | solution.py:25
  124.2 27.6 %collective-permute-start.4 = (bf16[36,64,128]{2,1,0:T(8,128)(2,1)S(1)}, bf16[36,64,128]{2,1,0:T(8,128)(2,1)S(1)}, u32[]{:S(2)}, u32[]{:S(2)}) collective-permute-start(bf16[36,64,128]{2,1,0:T(8,128)(2,1)S(1)} %bitcast.34), channel_id=1, source_target_pairs={{3,0},{7,4},{11,8},{15,12},{19,16},{23,20},{27,24},{31,28}} | collective-permute-start | bytes 1769480 | tf_op jit(solution)/shard_map/ppermute | solution.py:25

commit v3 on v2

--- a/solution.py
+++ b/solution.py
@@ -37,14 +37,31 @@
     return [value.astype(np.float32) for value in values]
 
 
-def dft_kernel(cos_ref, sin_ref, shift_cos_ref, shift_sin_ref, taper_ref, frames_ref, out_ref):
+def dft_kernel(tail, windows, offsets_ref, *refs):
+    cos_ref, sin_ref, shift_cos_ref, shift_sin_ref, taper_ref, record_ref, out_ref, padded = refs
     bin_count, block_length = cos_ref.shape
+    window_length, width = record_ref.shape
+    step = pl.program_id(0)
     shift_cos = shift_cos_ref[0]
     shift_sin = shift_sin_ref[0]
 
-    @pl.when(pl.program_id(0) == 0)
+    @pl.when(step == 0)
     def _():
         out_ref[...] = jnp.zeros_like(out_ref)
+
+        @pl.loop(0, window_length // block_length)
+        def _(number):
+            rows = pl.ds(pl.multiple_of(number * block_length, block_length), block_length)
+            loud = pl.ds(
+                pl.multiple_of(number * block_length + tail * window_length, block_length),
+                block_length,
+            )
+            silent = pl.ds(
+                pl.multiple_of(number * block_length + (1 - tail) * window_length, block_length),
+                block_length,
+            )
+            padded[loud, :] = record_ref[rows, :].astype(jnp.float32)
+            padded[silent, :] = jnp.zeros((block_length, width), jnp.float32)
 
     pieces = []
     for first in range(0, block_length, 256):
@@ -56,40 +73,46 @@
         sine = -tapering * (base_sin * shift_cos + base_cos * shift_sin)
         pieces.append(jnp.concatenate([cosine, sine], 0).astype(jnp.bfloat16))
     lookup = jnp.concatenate(pieces, 1)
-    width = frames_ref.shape[2]
-    for number in range(0, WPD, 2):
-        pair = jnp.concatenate([frames_ref[number], frames_ref[number + 1]], 1)
+    for number in range(0, len(windows), 2):
+        frames = []
+        for window in windows[number : number + 2]:
+            start = jnp.clip(offsets_ref[window], 0, window_length - 1)
+            rows = pl.ds(start + step * block_length, block_length)
+            frames.append(padded[rows, :].astype(jnp.bfloat16))
         out_ref[:, number * width : (number + 2) * width] += jnp.dot(
-            lookup, pair, preferred_element_type=jnp.float32
+            lookup, jnp.concatenate(frames, 1), preferred_element_type=jnp.float32
         )
 
 
-def transform(frames):
-    count, window_length, width = frames.shape
+def transform(record, offsets, tail, windows):
+    window_length, width = record.shape
+    count = len(windows)
     block_length = math.gcd(window_length, 1024)
     bin_count = KEEP + 2 * HALF
     steps = window_length // block_length
     return pl.pallas_call(
-        dft_kernel,
+        functools.partial(dft_kernel, tail, windows),
         grid=(steps,),
         in_specs=[
+            pl.BlockSpec(memory_space=pltpu.SMEM),
             pl.BlockSpec((bin_count, block_length), lambda i: (0, 0)),
             pl.BlockSpec((bin_count, block_length), lambda i: (0, 0)),
             pl.BlockSpec((1, bin_count, 1), lambda i: (i, 0, 0)),
             pl.BlockSpec((1, bin_count, 1), lambda i: (i, 0, 0)),
             pl.BlockSpec((1, 1, block_length), lambda i: (i, 0, 0)),
-            pl.BlockSpec((count, block_length, width), lambda i: (0, i, 0)),
+            pl.BlockSpec((window_length, width), lambda i: (0, 0)),
         ],
         out_specs=pl.BlockSpec((2 * bin_count, count * width), lambda i: (0, 0)),
         out_shape=jax.ShapeDtypeStruct((2 * bin_count, count * width), jnp.float32),
-        compiler_params=pltpu.CompilerParams(vmem_limit_bytes=40 * 2**20),
+        scratch_shapes=[pltpu.VMEM((2 * window_length, width), jnp.float32)],
+        compiler_params=pltpu.CompilerParams(vmem_limit_bytes=44 * 2**20),
         cost_estimate=pl.CostEstimate(
             flops=4 * bin_count * count * width * window_length,
-            bytes_accessed=2 * count * width * window_length,
+            bytes_accessed=2 * width * window_length,
             transcendentals=0,
         ),
         name="windowed_transform",
-    )(*base_tables(window_length, block_length), frames)
+    )(offsets, *base_tables(window_length, block_length), record)
 
 
 def smoother_matrix():
@@ -166,27 +189,20 @@
     )(*pieces)
 
 
-def cut(joined, offsets, window_length):
-    return jnp.stack(
-        [
-            lax.dynamic_slice_in_dim(joined, offsets[number], window_length, 0)
-            for number in range(WPD)
-        ]
-    )
-
-
 def local(record, window_starts, alive_mask):
     window_length = record.shape[0]
     local_width = record.shape[1]
     index_time = lax.axis_index("tm")
     offsets = window_starts - index_time * window_length
     earlier_offsets = passed_along(offsets, "tm", 1)
-    silence = jnp.zeros_like(record)
-    tails = cut(jnp.concatenate([silence, record], 0), earlier_offsets, window_length)
-    tail_spectra = transform(tails)
-    following = passed_along(tail_spectra, "tm", -1)
-    heads = cut(jnp.concatenate([record, silence], 0), offsets, window_length)
-    spectra = transform(heads) + following
+    all_windows = tuple(range(WPD))
+    heads = transform(record, offsets, 0, all_windows)
+    heads, earlier_offsets = lax.optimization_barrier((heads, earlier_offsets))
+    arrived = []
+    for windows in (all_windows[: WPD // 2], all_windows[WPD // 2 :]):
+        tails = transform(record, earlier_offsets, 1, windows)
+        arrived.append(passed_along(tails, "tm", -1))
+    spectra = heads + jnp.concatenate(arrived, 1)
     whitened = whiten(spectra, alive_mask)
     regrouped = lax.all_to_all(whitened, "tm", split_axis=0, concat_axis=1, tiled=True)
     reach_count = BAND // local_width

time: 172 us -> 162 us (0.942)
  the two profiles are of different devices: /device:TPU:0 before, /device:TPU:1 now
where the time goes in v3:
time: 162 us; the launch traced here: 161 us
  Pallas kernels  61.5 us (38%)
  waiting for transfers between devices  57.2 us (35%)
  blocking collectives  19.7 us (12%)
  starting transfers between devices  13.5 us (8%)
  local copies, waits for them, and re-layouts  7.05 us (4%)
    ppermute x6, waiting for transfers between devices, passed_along(): return lax.ppermute(block, axis, route)  57.2 us
    pallas_call x3, Pallas kernels, transform(): pl.pallas_call(functools.partial(dft_kernel, tail, windows), grid=(steps,...  42.8 us
    all_to_all x1, blocking collectives, local(): lax.all_to_all(whitened, 'tm', split_axis=0, concat_axis=1, tiled=True)  19.7 us
    pallas_call x1, Pallas kernels, stacked_bands(): pl.pallas_call(functools.partial(gram_kernel, len(pieces)), grid=(bins //...  18.7 us
    ppermute x6, starting transfers between devices, passed_along(): return lax.ppermute(block, axis, route)  13.5 us
    unnamed x14, local copies, waits for them, and re-layouts  6.75 us
  transfers between devices with their start and end apart: 6, of which 4 were waited for; matrix products, arithmetic and copies ran while one was open for 0% of the time, Pallas kernels for 11%

profile of v3, /device:TPU:1, one launch (start us, length us, event | category | flops | bytes accessed | tf_op | source)
XLA Modules:
  0.0 161.4 jit_solution(10403197372454015905)
XLA Ops:
  0.0 0.7 broadcast_subtract_fusion.offsets_ref
  0.7 3.9 %collective-permute-start = (s32[4]{0:T(128)S(1)}, s32[4]{0:T(128)S(1)}, u32[]{:S(2)}, u32[]{:S(2)}) collective-permute-start(s32[4]{0:T(128)S(1)} %broadcast_subtract_fusion.offsets_ref), channel_id=1, source_target_pairs={{0,4},{4,8},{8,12},{12,16},{16,20},{20,24},{24,28},{1,5},{5,9},{9,... | collective-permute-start | bytes 56 | tf_op jit(solution)/shard_map/ppermute | solution.py:25
  4.6 1.6 copy-done
  6.2 1.6 copy-done.2
  7.8 1.4 copy-done.3
  9.2 1.4 copy-done.4
  10.6 0.8 copy-done.5
  11.3 17.3 %windowed_transform.3 = f32[704,512]{1,0:T(8,128)S(1)} custom-call(s32[4]{0:T(128)S(1)} %broadcast_subtract_fusion.offsets_ref, f32[352,1024]{1,0:T(8,128)S(1)} %copy-done.4, f32[352,1024]{1,0:T(8,128)S(1)} %copy-done.3, f32[12,352,1]{2,1,0:T(8,128)S(1)} %copy-done.2, f32[12,352,1]{2,1,0:T(8,128)S(1)} %copy-done, f32[12,1,1024]{2,1,0:T(1,128)S(1)} %copy-done.5, ...), custom_call_target="tpu_custom_call" | custom-call | flops 8858370048 | bytes 3145728 | tf_op jit(solution)/shard_map/windowed_transform/pallas_call | solution.py:93
  28.6 12.8 %windowed_transform.5 = f32[704,256]{1,0:T(8,128)S(1)} custom-call(s32[4]{0:T(128)S(1)} %collective-permute-done.offsets_ref, f32[352,1024]{1,0:T(8,128)S(1)} %copy-done.4, f32[352,1024]{1,0:T(8,128)S(1)} %copy-done.3, f32[12,352,1]{2,1,0:T(8,128)S(1)} %copy-done.2, f32[12,352,1]{2,1,0:T(8,128)S(1)} %copy-done.1, f32[12,1,1024]{2,1,0:T(1,128)S(1)} %copy-done.5, ...), custom_call_target="tpu_custom_call" | custom-call | flops 4429185024 | bytes 3145728 | tf_op jit(solution)/shard_map/windowed_transform/pallas_call | solution.py:93
  41.4 12.8 %windowed_transform.4 = f32[704,256]{1,0:T(8,128)S(1)} custom-call(s32[4]{0:T(128)S(1)} %collective-permute-done.offsets_ref, f32[352,1024]{1,0:T(8,128)S(1)} %copy-done.4, f32[352,1024]{1,0:T(8,128)S(1)} %copy-done.3, f32[12,352,1]{2,1,0:T(8,128)S(1)} %copy-done.2, f32[12,352,1]{2,1,0:T(8,128)S(1)} %copy-done.1, f32[12,1,1024]{2,1,0:T(1,128)S(1)} %copy-done.5, ...), custom_call_target="tpu_custom_call" | custom-call | flops 4429185024 | bytes 3145728 | tf_op jit(solution)/shard_map/windowed_transform/pallas_call | solution.py:93
  54.2 1.3 collective-permute-start.1
  55.5 1.3 collective-permute-start.2
  56.9 16.8 %collective-permute-done.1 = f32[704,256]{1,0:T(8,128)S(1)} collective-permute-done((f32[704,256]{1,0:T(8,128)S(1)}, f32[704,256]{1,0:T(8,128)S(1)}, u32[]{:S(2)}, u32[]{:S(2)}) %collective-permute-start.1) | collective-permute-done | bytes 720928 | tf_op jit(solution)/shard_map/ppermute | solution.py:25
  73.7 15.4 %collective-permute-done.2 = f32[704,256]{1,0:T(8,128)S(1)} collective-permute-done((f32[704,256]{1,0:T(8,128)S(1)}, f32[704,256]{1,0:T(8,128)S(1)}, u32[]{:S(2)}, u32[]{:S(2)}) %collective-permute-start.2) | collective-permute-done | bytes 720928 | tf_op jit(solution)/shard_map/ppermute | solution.py:25
  89.1 0.3 maximum_add_fusion
  89.4 1.0 fusion.6
  90.6 0.3 pad_maximum_fusion
  90.9 19.7 %all_to_all.18 = bf16[288,8,128]{2,1,0:T(8,128)(2,1)S(1)} all-to-all(bf16[288,8,128]{2,1,0:T(8,128)(2,1)S(1)} %pad_maximum_fusion), channel_id=1, replica_groups=mesh['tm'=8,'chan'=4] {'tm'}, dimensions={0} | all-to-all | bytes 1179648 | tf_op jit(solution)/shard_map/all_to_all | solution.py:207
  110.8 0.7 collective-permute-start.5
  111.5 1.3 collective-permute-start.4
  112.8 5.0 %collective-permute-start.3 = (bf16[36,64,128]{2,1,0:T(8,128)(2,1)S(1)}, bf16[36,64,128]{2,1,0:T(8,128)(2,1)S(1)}, u32[]{:S(2)}, u32[]{:S(2)}) collective-permute-start(bf16[36,64,128]{2,1,0:T(8,128)(2,1)S(1)} %bitcast.10), channel_id=1, source_target_pairs={{1,0},{2,1},{3,2},{5,4},{6,5},{7,6},{9,8},{10,9},{11,10},{13,12},{... | collective-permute-start | bytes 1769480 | tf_op jit(solution)/shard_map/ppermute | solution.py:25
  117.8 23.0 %collective-permute-done.4.refs_2_ = bf16[36,64,128]{2,1,0:T(8,128)(2,1)S(1)} collective-permute-done((bf16[36,64,128]{2,1,0:T(8,128)(2,1)S(1)}, bf16[36,64,128]{2,1,0:T(8,128)(2,1)S(1)}, u32[]{:S(2)}, u32[]{:S(2)}) %collective-permute-start.4) | collective-permute-done | bytes 589856 | tf_op jit(solution)/shard_map/ppermute | solution.py:25
  140.8 1.9 %collective-permute-done.3.refs_1_ = bf16[36,64,128]{2,1,0:T(8,128)(2,1)S(1)} collective-permute-done((bf16[36,64,128]{2,1,0:T(8,128)(2,1)S(1)}, bf16[36,64,128]{2,1,0:T(8,128)(2,1)S(1)}, u32[]{:S(2)}, u32[]{:S(2)}) %collective-permute-start.3) | collective-permute-done | bytes 589856 | tf_op jit(solution)/shard_map/ppermute | solution.py:25
  142.7 18.7 %stacked_bands.1 = f32[2,36,128,512]{3,2,1,0:T(8,128)} custom-call(bf16[36,64,128]{2,1,0:T(8,128)(2,1)S(1)} %bitcast.11, bf16[36,64,128]{2,1,0:T(8,128)(2,1)S(1)} %collective-permute-done.3.refs_1_, bf16[36,64,128]{2,1,0:T(8,128)(2,1)S(1)} %collective-permute-done.4.refs_2_, bf16[36,64,128]{2,1,0:T(8,128)(2,1)S(1)} %collective-permute-done.5.refs_3_), custom_call_target="tpu_custom_call" | custom-call | tf_op jit(solution)/shard_map/stacked_bands/pallas_call | solution.py:181
  (17 shorter events, 0.3 us)
Async XLA Ops:
  0.7 28.0 %collective-permute-start = (s32[4]{0:T(128)S(1)}, s32[4]{0:T(128)S(1)}, u32[]{:S(2)}, u32[]{:S(2)}) collective-permute-start(s32[4]{0:T(128)S(1)} %broadcast_subtract_fusion.offsets_ref), channel_id=1, source_target_pairs={{0,4},{4,8},{8,12},{12,16},{16,20},{20,24},{24,28},{1,5},{5,9},{9,... | collective-permute-start | bytes 56 | tf_op jit(solution)/shard_map/ppermute | solution.py:25
  4.6 1.6 copy-start
  6.2 1.6 copy-start.2
  7.8 1.4 copy-start.3
  9.2 1.4 copy-start.4
  10.5 0.8 copy-start.5
  11.3 17.3 %copy-start.1 = (f32[12,352,1]{2,1,0:T(8,128)S(1)}, f32[12,352,1]{2,1,0:T(8,128)}, u32[]{:S(2)}) copy-start(f32[12,352,1]{2,1,0:T(8,128)} %constant.28.clone.refs_3_) | copy-start | bytes 50692
  41.4 15.4 %copy-start.6 = (s32[128]{0:T(128)S(1)}, s32[128]{0:T(128)}, u32[]{:S(2)}) copy-start(s32[128]{0:T(128)} %param.20) | copy-start | bytes 1540
  54.2 19.4 %collective-permute-start.1 = (f32[704,256]{1,0:T(8,128)S(1)}, f32[704,256]{1,0:T(8,128)S(1)}, u32[]{:S(2)}, u32[]{:S(2)}) collective-permute-start(f32[704,256]{1,0:T(8,128)S(1)} %windowed_transform.4), channel_id=1, source_target_pairs={{4,0},{8,4},{12,8},{16,12},{20,16},{24,20},{28,24},{5,1},{9,5},{13... | collective-permute-start | bytes 2162696 | tf_op jit(solution)/shard_map/ppermute | solution.py:25
  55.5 33.6 %collective-permute-start.2 = (f32[704,256]{1,0:T(8,128)S(1)}, f32[704,256]{1,0:T(8,128)S(1)}, u32[]{:S(2)}, u32[]{:S(2)}) collective-permute-start(f32[704,256]{1,0:T(8,128)S(1)} %windowed_transform.5), channel_id=1, source_target_pairs={{4,0},{8,4},{12,8},{16,12},{20,16},{24,20},{28,24},{5,1},{9,5},{13... | collective-permute-start | bytes 2162696 | tf_op jit(solution)/shard_map/ppermute | solution.py:25
  110.8 7.0 %collective-permute-start.5 = (bf16[36,64,128]{2,1,0:T(8,128)(2,1)S(1)}, bf16[36,64,128]{2,1,0:T(8,128)(2,1)S(1)}, u32[]{:S(2)}, u32[]{:S(2)}) collective-permute-start(bf16[36,64,128]{2,1,0:T(8,128)(2,1)S(1)} %bitcast.8), channel_id=1, source_target_pairs={{3,0},{7,4},{11,8},{15,12},{19,16},{23,20},{27,24},{31,28}} | collective-permute-start | bytes 1769480 | tf_op jit(solution)/shard_map/ppermute | solution.py:25
  111.5 29.3 %collective-permute-start.4 = (bf16[36,64,128]{2,1,0:T(8,128)(2,1)S(1)}, bf16[36,64,128]{2,1,0:T(8,128)(2,1)S(1)}, u32[]{:S(2)}, u32[]{:S(2)}) collective-permute-start(bf16[36,64,128]{2,1,0:T(8,128)(2,1)S(1)} %bitcast.9), channel_id=1, source_target_pairs={{2,0},{3,1},{6,4},{7,5},{10,8},{11,9},{14,12},{15,13},{18,16},{19,... | collective-permute-start | bytes 1769480 | tf_op jit(solution)/shard_map/ppermute | solution.py:25
  112.8 29.9 %collective-permute-start.3 = (bf16[36,64,128]{2,1,0:T(8,128)(2,1)S(1)}, bf16[36,64,128]{2,1,0:T(8,128)(2,1)S(1)}, u32[]{:S(2)}, u32[]{:S(2)}) collective-permute-start(bf16[36,64,128]{2,1,0:T(8,128)(2,1)S(1)} %bitcast.10), channel_id=1, source_target_pairs={{1,0},{2,1},{3,2},{5,4},{6,5},{7,6},{9,8},{10,9},{11,10},{13,12},{... | collective-permute-start | bytes 1769480 | tf_op jit(solution)/shard_map/ppermute | solution.py:25

commit v4 on v3

--- a/solution.py
+++ b/solution.py
@@ -196,13 +196,9 @@
     offsets = window_starts - index_time * window_length
     earlier_offsets = passed_along(offsets, "tm", 1)
     all_windows = tuple(range(WPD))
-    heads = transform(record, offsets, 0, all_windows)
-    heads, earlier_offsets = lax.optimization_barrier((heads, earlier_offsets))
-    arrived = []
-    for windows in (all_windows[: WPD // 2], all_windows[WPD // 2 :]):
-        tails = transform(record, earlier_offsets, 1, windows)
-        arrived.append(passed_along(tails, "tm", -1))
-    spectra = heads + jnp.concatenate(arrived, 1)
+    tails = transform(record, earlier_offsets, 1, all_windows)
+    following = passed_along(tails, "tm", -1)
+    spectra = transform(record, offsets, 0, all_windows) + following
     whitened = whiten(spectra, alive_mask)
     regrouped = lax.all_to_all(whitened, "tm", split_axis=0, concat_axis=1, tiled=True)
     reach_count = BAND // local_width

time: 162 us -> 135 us (0.83)
  waiting for transfers between devices: 57.2 us -> 42.7 us
  Pallas kernels: 61.5 us -> 50.3 us
    ppermute x6 -> x5, waiting for transfers between devices: 57.2 us -> 42.7 us  [passed_along(): return lax.ppermute(block, axis, route)]
    pallas_call x3 -> x2, Pallas kernels: 42.8 us -> 31.7 us  [transform(): pl.pallas_call(functools.partial(dft_kernel, tail, windows), grid=(steps,...]
    ppermute x6 -> x5, starting transfers between devices: 13.5 us -> 12.3 us  [passed_along(): return lax.ppermute(block, axis, route)]
    unnamed x14 -> x18, local copies, waits for them, and re-layouts: 6.75 us -> 6.75 us
  transfers between devices with their start and end apart: 6 -> 5, of which waited for: 4 -> 4; matrix products, arithmetic and copies ran while one was open for 0% -> 0% of each run, Pallas kernels for 11% -> 12%
where the time goes in v4:
time: 135 us
  Pallas kernels  50.3 us (37%)
  waiting for transfers between devices  42.7 us (32%)
  blocking collectives  20 us (15%)
  starting transfers between devices  12.3 us (9%)
  local copies, waits for them, and re-layouts  7.06 us (5%)
    ppermute x5, waiting for transfers between devices, passed_along(): return lax.ppermute(block, axis, route)  42.7 us
    pallas_call x2, Pallas kernels, transform(): pl.pallas_call(functools.partial(dft_kernel, tail, windows), grid=(steps,...  31.7 us
    all_to_all x1, blocking collectives, local(): lax.all_to_all(whitened, 'tm', split_axis=0, concat_axis=1, tiled=True)  20 us
    pallas_call x1, Pallas kernels, stacked_bands(): pl.pallas_call(functools.partial(gram_kernel, len(pieces)), grid=(bins //...  18.6 us
    ppermute x5, starting transfers between devices, passed_along(): return lax.ppermute(block, axis, route)  12.3 us
    unnamed x18, local copies, waits for them, and re-layouts  6.75 us
  transfers between devices with their start and end apart: 5, of which 4 were waited for; matrix products, arithmetic and copies ran while one was open for 0% of the time, Pallas kernels for 12%

profile of v4, /device:TPU:1, one launch (start us, length us, event | category | flops | bytes accessed | tf_op | source)
XLA Modules:
  0.0 134.8 jit_solution(14537260652141559153)
XLA Ops:
  0.0 0.7 broadcast_subtract_fusion.offsets_ref
  0.7 3.9 %collective-permute-start = (s32[4]{0:T(128)S(1)}, s32[4]{0:T(128)S(1)}, u32[]{:S(2)}, u32[]{:S(2)}) collective-permute-start(s32[4]{0:T(128)S(1)} %broadcast_subtract_fusion.offsets_ref), channel_id=1, source_target_pairs={{0,4},{4,8},{8,12},{12,16},{16,20},{20,24},{24,28},{1,5},{5,9},{9,... | collective-permute-start | bytes 56 | tf_op jit(solution)/shard_map/ppermute | solution.py:25
  4.6 0.7 collective-permute-done.offsets_ref
  5.3 1.6 %copy-done = f32[12,352,1]{2,1,0:T(8,128)S(1)} copy-done((f32[12,352,1]{2,1,0:T(8,128)S(1)}, f32[12,352,1]{2,1,0:T(8,128)}, u32[]{:S(2)}) %copy-start) | copy-done | bytes 16920
  6.9 1.6 %copy-done.2 = f32[12,352,1]{2,1,0:T(8,128)S(1)} copy-done((f32[12,352,1]{2,1,0:T(8,128)S(1)}, f32[12,352,1]{2,1,0:T(8,128)}, u32[]{:S(2)}) %copy-start.2) | copy-done | bytes 16920
  8.5 1.4 %copy-done.4 = f32[352,1024]{1,0:T(8,128)S(1)} copy-done((f32[352,1024]{1,0:T(8,128)S(1)}, f32[352,1024]{1,0:T(8,128)}, u32[]{:S(2)}) %copy-start.4) | copy-done | bytes 1441816
  9.9 1.4 %copy-done.6 = f32[352,1024]{1,0:T(8,128)S(1)} copy-done((f32[352,1024]{1,0:T(8,128)S(1)}, f32[352,1024]{1,0:T(8,128)}, u32[]{:S(2)}) %copy-start.6) | copy-done | bytes 1441816
  11.3 0.8 copy-done.7
  12.1 15.3 %windowed_transform.3 = f32[704,512]{1,0:T(8,128)S(1)} custom-call(s32[4]{0:T(128)S(1)} %collective-permute-done.offsets_ref, f32[352,1024]{1,0:T(8,128)S(1)} %copy-done.6, f32[352,1024]{1,0:T(8,128)S(1)} %copy-done.4, f32[12,352,1]{2,1,0:T(8,128)S(1)} %copy-done.2, f32[12,352,1]{2,1,0:T(8,128)S(1)} %copy-done, f32[12,1,1024]{2,1,0:T(1,128)S(1)} %copy-done.7, ...), custom_call_target="tpu_custom_call" | custom-call | flops 8858370048 | bytes 3145728 | tf_op jit(solution)/shard_map/windowed_transform/pallas_call | solution.py:93
  27.4 1.3 collective-permute-start.1
  28.7 16.4 %windowed_transform.2 = f32[704,512]{1,0:T(8,128)S(1)} custom-call(s32[4]{0:T(128)S(1)} %broadcast_subtract_fusion.offsets_ref, f32[352,1024]{1,0:T(8,128)S(1)} %copy-done.6, f32[352,1024]{1,0:T(8,128)S(1)} %copy-done.5, f32[12,352,1]{2,1,0:T(8,128)S(1)} %copy-done.3, f32[12,352,1]{2,1,0:T(8,128)S(1)} %copy-done.1, f32[12,1,1024]{2,1,0:T(1,128)S(1)} %copy-done.7, ...), custom_call_target="tpu_custom_call" | custom-call | flops 8858370048 | bytes 3145728 | tf_op jit(solution)/shard_map/windowed_transform/pallas_call | solution.py:93
  45.1 17.0 %collective-permute-done.1 = f32[704,512]{1,0:T(8,128)S(1)} collective-permute-done((f32[704,512]{1,0:T(8,128)S(1)}, f32[704,512]{1,0:T(8,128)S(1)}, u32[]{:S(2)}, u32[]{:S(2)}) %collective-permute-start.1) | collective-permute-done | bytes 1441824 | tf_op jit(solution)/shard_map/ppermute | solution.py:25
  62.1 0.3 add.23
  62.5 1.0 fusion.6
  63.6 0.1 concatenate.10
  63.6 0.3 pad_maximum_fusion
  64.0 20.0 %all_to_all.18 = bf16[288,8,128]{2,1,0:T(8,128)(2,1)S(1)} all-to-all(bf16[288,8,128]{2,1,0:T(8,128)(2,1)S(1)} %pad_maximum_fusion), channel_id=1, replica_groups=mesh['tm'=8,'chan'=4] {'tm'}, dimensions={0} | all-to-all | bytes 1179648 | tf_op jit(solution)/shard_map/all_to_all | solution.py:203
  83.9 0.2 copy.16
  84.1 0.7 collective-permute-start.4
  84.8 1.3 collective-permute-start.3
  86.1 5.1 %collective-permute-start.2 = (bf16[36,64,128]{2,1,0:T(8,128)(2,1)S(1)}, bf16[36,64,128]{2,1,0:T(8,128)(2,1)S(1)}, u32[]{:S(2)}, u32[]{:S(2)}) collective-permute-start(bf16[36,64,128]{2,1,0:T(8,128)(2,1)S(1)} %bitcast.10), channel_id=1, source_target_pairs={{1,0},{2,1},{3,2},{5,4},{6,5},{7,6},{9,8},{10,9},{11,10},{13,12},{... | collective-permute-start | bytes 1769480 | tf_op jit(solution)/shard_map/ppermute | solution.py:25
  91.2 23.0 %collective-permute-done.3.refs_2_ = bf16[36,64,128]{2,1,0:T(8,128)(2,1)S(1)} collective-permute-done((bf16[36,64,128]{2,1,0:T(8,128)(2,1)S(1)}, bf16[36,64,128]{2,1,0:T(8,128)(2,1)S(1)}, u32[]{:S(2)}, u32[]{:S(2)}) %collective-permute-start.3) | collective-permute-done | bytes 589856 | tf_op jit(solution)/shard_map/ppermute | solution.py:25
  114.2 1.9 %collective-permute-done.2.refs_1_ = bf16[36,64,128]{2,1,0:T(8,128)(2,1)S(1)} collective-permute-done((bf16[36,64,128]{2,1,0:T(8,128)(2,1)S(1)}, bf16[36,64,128]{2,1,0:T(8,128)(2,1)S(1)}, u32[]{:S(2)}, u32[]{:S(2)}) %collective-permute-start.2) | collective-permute-done | bytes 589856 | tf_op jit(solution)/shard_map/ppermute | solution.py:25
  116.2 18.6 %stacked_bands.1 = f32[2,36,128,512]{3,2,1,0:T(8,128)} custom-call(bf16[36,64,128]{2,1,0:T(8,128)(2,1)S(1)} %bitcast.11, bf16[36,64,128]{2,1,0:T(8,128)(2,1)S(1)} %collective-permute-done.2.refs_1_, bf16[36,64,128]{2,1,0:T(8,128)(2,1)S(1)} %collective-permute-done.3.refs_2_, bf16[36,64,128]{2,1,0:T(8,128)(2,1)S(1)} %collective-permute-done.4.refs_3_), custom_call_target="tpu_custom_call" | custom-call | tf_op jit(solution)/shard_map/stacked_bands/pallas_call | solution.py:181
  (18 shorter events, 0.1 us)
Async XLA Ops:
  0.0 28.7 %copy-start.8 = (s32[128]{0:T(128)S(1)}, s32[128]{0:T(128)}, u32[]{:S(2)}) copy-start(s32[128]{0:T(128)} %param.15) | copy-start | bytes 1540
  0.7 4.6 %collective-permute-start = (s32[4]{0:T(128)S(1)}, s32[4]{0:T(128)S(1)}, u32[]{:S(2)}, u32[]{:S(2)}) collective-permute-start(s32[4]{0:T(128)S(1)} %broadcast_subtract_fusion.offsets_ref), channel_id=1, source_target_pairs={{0,4},{4,8},{8,12},{12,16},{16,20},{20,24},{24,28},{1,5},{5,9},{9,... | collective-permute-start | bytes 56 | tf_op jit(solution)/shard_map/ppermute | solution.py:25
  5.3 1.6 %copy-start = (f32[12,352,1]{2,1,0:T(8,128)S(1)}, f32[12,352,1]{2,1,0:T(8,128)}, u32[]{:S(2)}) copy-start(f32[12,352,1]{2,1,0:T(8,128)} %constant.28.clone.refs_3_) | copy-start | bytes 50692
  6.9 1.6 %copy-start.2 = (f32[12,352,1]{2,1,0:T(8,128)S(1)}, f32[12,352,1]{2,1,0:T(8,128)}, u32[]{:S(2)}) copy-start(f32[12,352,1]{2,1,0:T(8,128)} %constant.27.clone.refs_2_) | copy-start | bytes 50692
  8.5 1.4 %copy-start.4 = (f32[352,1024]{1,0:T(8,128)S(1)}, f32[352,1024]{1,0:T(8,128)}, u32[]{:S(2)}) copy-start(f32[352,1024]{1,0:T(8,128)} %constant.26.clone.refs_1_) | copy-start | bytes 4325380
  9.9 1.4 %copy-start.6 = (f32[352,1024]{1,0:T(8,128)S(1)}, f32[352,1024]{1,0:T(8,128)}, u32[]{:S(2)}) copy-start(f32[352,1024]{1,0:T(8,128)} %constant.25.clone.refs_0_) | copy-start | bytes 4325380
  11.3 0.8 copy-start.7
  12.1 16.6 %copy-start.1 = (f32[12,352,1]{2,1,0:T(8,128)S(1)}, f32[12,352,1]{2,1,0:T(8,128)}, u32[]{:S(2)}) copy-start(f32[12,352,1]{2,1,0:T(8,128)} %constant.28.clone.refs_3_) | copy-start | bytes 50692
  12.1 16.7 %copy-start.3 = (f32[12,352,1]{2,1,0:T(8,128)S(1)}, f32[12,352,1]{2,1,0:T(8,128)}, u32[]{:S(2)}) copy-start(f32[12,352,1]{2,1,0:T(8,128)} %constant.27.clone.refs_2_) | copy-start | bytes 50692
  12.1 16.7 %copy-start.5 = (f32[352,1024]{1,0:T(8,128)S(1)}, f32[352,1024]{1,0:T(8,128)}, u32[]{:S(2)}) copy-start(f32[352,1024]{1,0:T(8,128)} %constant.26.clone.refs_1_) | copy-start | bytes 4325380
  27.4 34.8 %collective-permute-start.1 = (f32[704,512]{1,0:T(8,128)S(1)}, f32[704,512]{1,0:T(8,128)S(1)}, u32[]{:S(2)}, u32[]{:S(2)}) collective-permute-start(f32[704,512]{1,0:T(8,128)S(1)} %windowed_transform.3), channel_id=1, source_target_pairs={{4,0},{8,4},{12,8},{16,12},{20,16},{24,20},{28,24},{5,1},{9,5},{13... | collective-permute-start | bytes 4325384 | tf_op jit(solution)/shard_map/ppermute | solution.py:25
  84.1 7.1 %collective-permute-start.4 = (bf16[36,64,128]{2,1,0:T(8,128)(2,1)S(1)}, bf16[36,64,128]{2,1,0:T(8,128)(2,1)S(1)}, u32[]{:S(2)}, u32[]{:S(2)}) collective-permute-start(bf16[36,64,128]{2,1,0:T(8,128)(2,1)S(1)} %bitcast.8), channel_id=1, source_target_pairs={{3,0},{7,4},{11,8},{15,12},{19,16},{23,20},{27,24},{31,28}} | collective-permute-start | bytes 1769480 | tf_op jit(solution)/shard_map/ppermute | solution.py:25
  84.8 29.5 %collective-permute-start.3 = (bf16[36,64,128]{2,1,0:T(8,128)(2,1)S(1)}, bf16[36,64,128]{2,1,0:T(8,128)(2,1)S(1)}, u32[]{:S(2)}, u32[]{:S(2)}) collective-permute-start(bf16[36,64,128]{2,1,0:T(8,128)(2,1)S(1)} %bitcast.9), channel_id=1, source_target_pairs={{2,0},{3,1},{6,4},{7,5},{10,8},{11,9},{14,12},{15,13},{18,16},{19,... | collective-permute-start | bytes 1769480 | tf_op jit(solution)/shard_map/ppermute | solution.py:25
  86.1 30.1 %collective-permute-start.2 = (bf16[36,64,128]{2,1,0:T(8,128)(2,1)S(1)}, bf16[36,64,128]{2,1,0:T(8,128)(2,1)S(1)}, u32[]{:S(2)}, u32[]{:S(2)}) collective-permute-start(bf16[36,64,128]{2,1,0:T(8,128)(2,1)S(1)} %bitcast.10), channel_id=1, source_target_pairs={{1,0},{2,1},{3,2},{5,4},{6,5},{7,6},{9,8},{10,9},{11,10},{13,12},{... | collective-permute-start | bytes 1769480 | tf_op jit(solution)/shard_map/ppermute | solution.py:25

commit v5 on v4

--- a/solution.py
+++ b/solution.py
@@ -137,12 +137,128 @@
     return whitened.reshape(KEEP, 2 * WPD, width)
 
 
-def gram_kernel(piece_count, *refs):
-    pieces = refs[:piece_count]
-    out_ref = refs[piece_count]
-    bins, rows, width = pieces[0].shape
+def gather_kernel(time_count, chan_count, white_ref, out_ref, sends, arrivals, hops, landings):
+    piece_count = out_ref.shape[0]
+    me_time = lax.axis_index("tm")
+    me_chan = lax.axis_index("chan")
+    below = lax.rem(me_chan + chan_count - 1, chan_count)
+    above = lax.rem(me_chan + 1, chan_count)
+
+    def signal(time, chan):
+        pl.semaphore_signal(
+            barrier, inc=1, device_id=(time, chan), device_id_type=pl.DeviceIdType.MESH
+        )
+
+    barrier = pltpu.get_barrier_semaphore()
+    for distance in range(1, time_count):
+        signal(lax.rem(me_time + distance, time_count), me_chan)
+    signal(me_time, below)
+    signal(me_time, above)
+    pl.semaphore_wait(barrier, time_count + 1)
+
+    def regroup(distance):
+        target = lax.rem(me_time + distance, time_count)
+        return pltpu.make_async_remote_copy(
+            src_ref=white_ref.at[target],
+            dst_ref=out_ref.at[0, me_time],
+            send_sem=sends.at[distance],
+            recv_sem=arrivals.at[distance],
+            device_id=(target, me_chan),
+            device_id_type=pl.DeviceIdType.MESH,
+        )
+
+    def source(distance):
+        return lax.rem(me_time - distance + time_count, time_count)
+
+    def arrival(distance):
+        return pltpu.make_async_remote_copy(
+            src_ref=white_ref.at[source(distance)],
+            dst_ref=out_ref.at[0, source(distance)],
+            send_sem=sends.at[distance],
+            recv_sem=arrivals.at[distance],
+            device_id=(source(distance), me_chan),
+            device_id_type=pl.DeviceIdType.MESH,
+        )
+
+    def hop(piece, distance):
+        return pltpu.make_async_remote_copy(
+            src_ref=out_ref.at[piece - 1, source(distance)],
+            dst_ref=out_ref.at[piece, source(distance)],
+            send_sem=hops.at[piece, distance],
+            recv_sem=landings.at[piece, distance],
+            device_id=(me_time, below),
+            device_id_type=pl.DeviceIdType.MESH,
+        )
+
+    for distance in range(1, time_count):
+        regroup(distance).start()
+    out_ref[0, me_time] = white_ref[me_time]
+
+    for turn in range(time_count + piece_count - 1):
+        for piece in range(piece_count):
+            distance = turn - piece
+            if not 0 <= distance < time_count:
+                continue
+            held = me_chan + piece < chan_count
+            if piece == 0:
+                if distance > 0:
+                    arrival(distance).wait_recv()
+            else:
+
+                @pl.when(held)
+                def _():
+                    hop(piece, distance).wait_recv()
+
+                @pl.when(~held)
+                def _():
+                    out_ref[piece, source(distance)] = jnp.zeros(
+                        out_ref.shape[2:], out_ref.dtype
+                    )
+
+            if piece + 1 < piece_count:
+
+                @pl.when(held & (me_chan > 0))
+                def _():
+                    hop(piece + 1, distance).start()
+
+    for distance in range(1, time_count):
+        regroup(distance).wait_send()
+    for piece in range(1, piece_count):
+        for distance in range(time_count):
+
+            @pl.when((me_chan + piece - 1 < chan_count) & (me_chan > 0))
+            def _():
+                hop(piece, distance).wait_send()
+
+
+def gather_pieces(whitened, piece_count):
+    time_count = lax.axis_size("tm")
+    chan_count = lax.axis_size("chan")
+    return pl.pallas_call(
+        functools.partial(gather_kernel, time_count, chan_count),
+        in_specs=[pl.BlockSpec(memory_space=pltpu.VMEM)],
+        out_specs=pl.BlockSpec(memory_space=pltpu.VMEM),
+        out_shape=jax.ShapeDtypeStruct((piece_count,) + whitened.shape, jnp.bfloat16),
+        scratch_shapes=[
+            pltpu.SemaphoreType.DMA((time_count,)),
+            pltpu.SemaphoreType.DMA((time_count,)),
+            pltpu.SemaphoreType.DMA((piece_count, time_count)),
+            pltpu.SemaphoreType.DMA((piece_count, time_count)),
+        ],
+        compiler_params=pltpu.CompilerParams(
+            collective_id=0, has_side_effects=True, vmem_limit_bytes=24 * 2**20
+        ),
+        name="gather_pieces",
+    )(whitened)
+
+
+def gram_kernel(pieces_ref, out_ref):
+    piece_count, time_count, _, width = pieces_ref.shape
+    bins = out_ref.shape[1]
     band = out_ref.shape[3]
+    rows = time_count * 2 * WPD
     window_count = rows // 2
+    groups = [pieces_ref[piece].astype(jnp.float32) for piece in range(piece_count)]
     row = lax.broadcasted_iota(jnp.int32, (rows, rows), 0)
     column = lax.broadcasted_iota(jnp.int32, (rows, rows), 1)
     first_half = row % 8 < 4
@@ -158,9 +274,13 @@
     contract = (((0,), (0,)), ((), ()))
     span = piece_count * width
     for f in range(bins):
-        own = jnp.dot(pieces[0][f], mirror, preferred_element_type=jnp.float32).astype(jnp.bfloat16)
+        pieces = [
+            group[:, f * 2 * WPD : (f + 1) * 2 * WPD].reshape(rows, width).astype(jnp.bfloat16)
+            for group in groups
+        ]
+        own = jnp.dot(pieces[0], mirror, preferred_element_type=jnp.float32).astype(jnp.bfloat16)
         rotated = jnp.dot(swap, own, preferred_element_type=jnp.float32).astype(jnp.bfloat16)
-        joined = jnp.concatenate([piece[f] for piece in pieces], 1)
+        joined = jnp.concatenate(pieces, 1)
         if span < band + width:
             joined = jnp.concatenate(
                 [joined, jnp.zeros((rows, band + width - span), jnp.bfloat16)], 1
@@ -176,17 +296,22 @@
 
 
 def stacked_bands(pieces):
-    bins, rows, width = pieces[0].shape
+    piece_count, time_count, rows, width = pieces.shape
+    bins = rows // (2 * WPD)
     block = 2
     return pl.pallas_call(
-        functools.partial(gram_kernel, len(pieces)),
+        gram_kernel,
         grid=(bins // block,),
-        in_specs=[pl.BlockSpec((block, rows, width), lambda i: (i, 0, 0))] * len(pieces),
+        in_specs=[
+            pl.BlockSpec(
+                (piece_count, time_count, block * 2 * WPD, width), lambda i: (0, 0, i, 0)
+            )
+        ],
         out_specs=pl.BlockSpec((2, block, width, BAND), lambda i: (0, i, 0, 0)),
         out_shape=jax.ShapeDtypeStruct((2, bins, width, BAND), jnp.float32),
         compiler_params=pltpu.CompilerParams(vmem_limit_bytes=48 * 2**20),
         name="stacked_bands",
-    )(*pieces)
+    )(pieces)
 
 
 def local(record, window_starts, alive_mask):
@@ -200,12 +325,10 @@
     following = passed_along(tails, "tm", -1)
     spectra = transform(record, offsets, 0, all_windows) + following
     whitened = whiten(spectra, alive_mask)
-    regrouped = lax.all_to_all(whitened, "tm", split_axis=0, concat_axis=1, tiled=True)
-    reach_count = BAND // local_width
-    pieces = [regrouped]
-    for distance in range(1, min(reach_count + 1, lax.axis_size("chan"))):
-        pieces.append(passed_along(regrouped, "chan", -distance))
-    return stacked_bands(pieces)
+    time_count = lax.axis_size("tm")
+    blocks = whitened.reshape(time_count, KEEP // time_count * 2 * WPD, local_width)
+    piece_count = min(BAND // local_width + 1, lax.axis_size("chan"))
+    return stacked_bands(gather_pieces(blocks, piece_count))
 
 
 def solution(mesh):

time: 135 us -> 115 us (0.85)
  the two profiles are of different devices: /device:TPU:1 before, /device:TPU:17 now
where the time goes in v5:
time: 115 us; the launch traced here: 114 us
  Pallas kernels  83.3 us (72%)
  waiting for transfers between devices  16.5 us (14%)
  local copies, waits for them, and re-layouts  7.01 us (6%)
  starting transfers between devices  5.07 us (4%)
    pallas_call x2, Pallas kernels, transform(): pl.pallas_call(functools.partial(dft_kernel, tail, windows), grid=(steps,...  33.2 us
    pallas_call x1, Pallas kernels, gather_pieces(): pl.pallas_call(functools.partial(gather_kernel, time_count, chan_count),...  31.2 us
    pallas_call x1, Pallas kernels, stacked_bands(): pl.pallas_call(gram_kernel, grid=(bins // block,), in_specs=[pl.BlockSpec...  18.9 us
    ppermute x2, waiting for transfers between devices, passed_along(): return lax.ppermute(block, axis, route)  16.5 us
    unnamed x18, local copies, waits for them, and re-layouts  6.75 us
    ppermute x2, starting transfers between devices, passed_along(): return lax.ppermute(block, axis, route)  5.07 us
  transfers between devices with their start and end apart: 2, of which 2 were waited for; matrix products, arithmetic and copies ran while one was open for 0% of the time, Pallas kernels for 15%

profile of v5, /device:TPU:17, one launch (start us, length us, event | category | flops | bytes accessed | tf_op | source)
XLA Modules:
  0.0 114.2 jit_solution(13876858712836421527)
XLA Ops:
  0.0 0.0 copy-start.8
  0.0 0.7 broadcast_subtract_fusion.offsets_ref
  0.7 3.1 %collective-permute-start = (s32[4]{0:T(128)S(1)}, s32[4]{0:T(128)S(1)}, u32[]{:S(2)}, u32[]{:S(2)}) collective-permute-start(s32[4]{0:T(128)S(1)} %broadcast_subtract_fusion.offsets_ref), channel_id=1, source_target_pairs={{0,4},{4,8},{8,12},{12,16},{16,20},{20,24},{24,28},{1,5},{5,9},{9,... | collective-permute-start | bytes 56 | tf_op jit(solution)/shard_map/ppermute | solution.py:25
  3.8 2.1 %collective-permute-done.offsets_ref = s32[4]{0:T(128)S(1)} collective-permute-done((s32[4]{0:T(128)S(1)}, s32[4]{0:T(128)S(1)}, u32[]{:S(2)}, u32[]{:S(2)}) %collective-permute-start) | collective-permute-done | bytes 48 | tf_op jit(solution)/shard_map/ppermute | solution.py:25
  5.8 0.0 copy-start
  5.8 1.6 %copy-done = f32[12,352,1]{2,1,0:T(8,128)S(1)} copy-done((f32[12,352,1]{2,1,0:T(8,128)S(1)}, f32[12,352,1]{2,1,0:T(8,128)}, u32[]{:S(2)}) %copy-start) | copy-done | bytes 16920
  7.5 1.6 %copy-done.2 = f32[12,352,1]{2,1,0:T(8,128)S(1)} copy-done((f32[12,352,1]{2,1,0:T(8,128)S(1)}, f32[12,352,1]{2,1,0:T(8,128)}, u32[]{:S(2)}) %copy-start.2) | copy-done | bytes 16920
  9.1 1.4 %copy-done.4 = f32[352,1024]{1,0:T(8,128)S(1)} copy-done((f32[352,1024]{1,0:T(8,128)S(1)}, f32[352,1024]{1,0:T(8,128)}, u32[]{:S(2)}) %copy-start.4) | copy-done | bytes 1441816
  10.4 1.4 %copy-done.6 = f32[352,1024]{1,0:T(8,128)S(1)} copy-done((f32[352,1024]{1,0:T(8,128)S(1)}, f32[352,1024]{1,0:T(8,128)}, u32[]{:S(2)}) %copy-start.6) | copy-done | bytes 1441816
  11.8 0.8 copy-done.7
  12.6 16.6 %windowed_transform.3 = f32[704,512]{1,0:T(8,128)S(1)} custom-call(s32[4]{0:T(128)S(1)} %collective-permute-done.offsets_ref, f32[352,1024]{1,0:T(8,128)S(1)} %copy-done.6, f32[352,1024]{1,0:T(8,128)S(1)} %copy-done.4, f32[12,352,1]{2,1,0:T(8,128)S(1)} %copy-done.2, f32[12,352,1]{2,1,0:T(8,128)S(1)} %copy-done, f32[12,1,1024]{2,1,0:T(1,128)S(1)} %copy-done.7, ...), custom_call_target="tpu_custom_call" | custom-call | flops 8858370048 | bytes 3145728 | tf_op jit(solution)/shard_map/windowed_transform/pallas_call | solution.py:93
  29.2 2.0 %collective-permute-start.1 = (f32[704,512]{1,0:T(8,128)S(1)}, f32[704,512]{1,0:T(8,128)S(1)}, u32[]{:S(2)}, u32[]{:S(2)}) collective-permute-start(f32[704,512]{1,0:T(8,128)S(1)} %windowed_transform.3), channel_id=1, source_target_pairs={{4,0},{8,4},{12,8},{16,12},{20,16},{24,20},{28,24},{5,1},{9,5},{13... | collective-permute-start | bytes 4325384 | tf_op jit(solution)/shard_map/ppermute | solution.py:25
  31.2 0.0 copy-done.8
  31.2 0.0 copy-done.1
  31.2 0.0 copy-done.3
  31.2 0.0 copy-done.5
  31.2 16.6 %windowed_transform.2 = f32[704,512]{1,0:T(8,128)S(1)} custom-call(s32[4]{0:T(128)S(1)} %broadcast_subtract_fusion.offsets_ref, f32[352,1024]{1,0:T(8,128)S(1)} %copy-done.6, f32[352,1024]{1,0:T(8,128)S(1)} %copy-done.5, f32[12,352,1]{2,1,0:T(8,128)S(1)} %copy-done.3, f32[12,352,1]{2,1,0:T(8,128)S(1)} %copy-done.1, f32[12,1,1024]{2,1,0:T(1,128)S(1)} %copy-done.7, ...), custom_call_target="tpu_custom_call" | custom-call | flops 8858370048 | bytes 3145728 | tf_op jit(solution)/shard_map/windowed_transform/pallas_call | solution.py:93
  47.9 14.5 %collective-permute-done.1 = f32[704,512]{1,0:T(8,128)S(1)} collective-permute-done((f32[704,512]{1,0:T(8,128)S(1)}, f32[704,512]{1,0:T(8,128)S(1)}, u32[]{:S(2)}, u32[]{:S(2)}) %collective-permute-start.1) | collective-permute-done | bytes 1441824 | tf_op jit(solution)/shard_map/ppermute | solution.py:25
  62.3 0.3 add.23
  62.7 1.0 fusion.6
  63.7 0.1 pad_maximum_fusion
  63.8 0.3 convert_element_type.10.white_ref
  64.0 31.2 %gather_pieces.1.pieces_ref = bf16[4,8,288,128]{3,2,1,0:T(8,128)(2,1)S(1)} custom-call(bf16[8,288,128]{2,1,0:T(8,128)(2,1)S(1)} %convert_element_type.10.white_ref), custom_call_target="tpu_custom_call" | custom-call | tf_op jit(solution)/shard_map/gather_pieces/pallas_call | solution.py:237
  95.3 18.9 %stacked_bands.1 = f32[2,36,128,512]{3,2,1,0:T(8,128)} custom-call(bf16[4,8,288,128]{3,2,1,0:T(8,128)(2,1)S(1)} %gather_pieces.1.pieces_ref), custom_call_target="tpu_custom_call" | custom-call | tf_op jit(solution)/shard_map/stacked_bands/pallas_call | solution.py:302
  (10 shorter events, 0.0 us)
Async XLA Ops:
  0.0 31.2 %copy-start.8 = (s32[128]{0:T(128)S(1)}, s32[128]{0:T(128)}, u32[]{:S(2)}) copy-start(s32[128]{0:T(128)} %param.15) | copy-start | bytes 1540
  0.7 5.2 %collective-permute-start = (s32[4]{0:T(128)S(1)}, s32[4]{0:T(128)S(1)}, u32[]{:S(2)}, u32[]{:S(2)}) collective-permute-start(s32[4]{0:T(128)S(1)} %broadcast_subtract_fusion.offsets_ref), channel_id=1, source_target_pairs={{0,4},{4,8},{8,12},{12,16},{16,20},{20,24},{24,28},{1,5},{5,9},{9,... | collective-permute-start | bytes 56 | tf_op jit(solution)/shard_map/ppermute | solution.py:25
  5.8 1.6 %copy-start = (f32[12,352,1]{2,1,0:T(8,128)S(1)}, f32[12,352,1]{2,1,0:T(8,128)}, u32[]{:S(2)}) copy-start(f32[12,352,1]{2,1,0:T(8,128)} %constant.28.clone.refs_3_) | copy-start | bytes 50692
  7.5 1.6 %copy-start.2 = (f32[12,352,1]{2,1,0:T(8,128)S(1)}, f32[12,352,1]{2,1,0:T(8,128)}, u32[]{:S(2)}) copy-start(f32[12,352,1]{2,1,0:T(8,128)} %constant.27.clone.refs_2_) | copy-start | bytes 50692
  9.1 1.4 %copy-start.4 = (f32[352,1024]{1,0:T(8,128)S(1)}, f32[352,1024]{1,0:T(8,128)}, u32[]{:S(2)}) copy-start(f32[352,1024]{1,0:T(8,128)} %constant.26.clone.refs_1_) | copy-start | bytes 4325380
  10.4 1.4 %copy-start.6 = (f32[352,1024]{1,0:T(8,128)S(1)}, f32[352,1024]{1,0:T(8,128)}, u32[]{:S(2)}) copy-start(f32[352,1024]{1,0:T(8,128)} %constant.25.clone.refs_0_) | copy-start | bytes 4325380
  11.8 0.8 copy-start.7
  12.6 18.6 %copy-start.1 = (f32[12,352,1]{2,1,0:T(8,128)S(1)}, f32[12,352,1]{2,1,0:T(8,128)}, u32[]{:S(2)}) copy-start(f32[12,352,1]{2,1,0:T(8,128)} %constant.28.clone.refs_3_) | copy-start | bytes 50692
  12.6 18.6 %copy-start.3 = (f32[12,352,1]{2,1,0:T(8,128)S(1)}, f32[12,352,1]{2,1,0:T(8,128)}, u32[]{:S(2)}) copy-start(f32[12,352,1]{2,1,0:T(8,128)} %constant.27.clone.refs_2_) | copy-start | bytes 50692
  12.6 18.6 %copy-start.5 = (f32[352,1024]{1,0:T(8,128)S(1)}, f32[352,1024]{1,0:T(8,128)}, u32[]{:S(2)}) copy-start(f32[352,1024]{1,0:T(8,128)} %constant.26.clone.refs_1_) | copy-start | bytes 4325380
  29.2 33.1 %collective-permute-start.1 = (f32[704,512]{1,0:T(8,128)S(1)}, f32[704,512]{1,0:T(8,128)S(1)}, u32[]{:S(2)}, u32[]{:S(2)}) collective-permute-start(f32[704,512]{1,0:T(8,128)S(1)} %windowed_transform.3), channel_id=1, source_target_pairs={{4,0},{8,4},{12,8},{16,12},{20,16},{24,20},{28,24},{5,1},{9,5},{13... | collective-permute-start | bytes 4325384 | tf_op jit(solution)/shard_map/ppermute | solution.py:25

commit v6 on v5

--- a/solution.py
+++ b/solution.py
@@ -31,7 +31,7 @@
     times = np.arange(block_length)
     firsts = np.arange(0, window_length, block_length)
     base = step_angle * (bin_numbers[:, None] * times[None, :] % window_length)
-    shift = step_angle * (bin_numbers[None, :, None] * firsts[:, None, None] % window_length)
+    shift = step_angle * (bin_numbers[:, None] * firsts[None, :] % window_length)
     tapering = 0.5 - 0.5 * np.cos(step_angle * (firsts[:, None, None] + times[None, None, :]))
     values = (np.cos(base), np.sin(base), np.cos(shift), np.sin(shift), tapering)
     return [value.astype(np.float32) for value in values]
@@ -42,8 +42,9 @@
     bin_count, block_length = cos_ref.shape
     window_length, width = record_ref.shape
     step = pl.program_id(0)
-    shift_cos = shift_cos_ref[0]
-    shift_sin = shift_sin_ref[0]
+    chosen = lax.broadcasted_iota(jnp.int32, shift_cos_ref.shape, 1) == step
+    shift_cos = jnp.sum(jnp.where(chosen, shift_cos_ref[...], 0.0), 1, keepdims=True)
+    shift_sin = jnp.sum(jnp.where(chosen, shift_sin_ref[...], 0.0), 1, keepdims=True)
 
     @pl.when(step == 0)
     def _():
@@ -97,8 +98,8 @@
             pl.BlockSpec(memory_space=pltpu.SMEM),
             pl.BlockSpec((bin_count, block_length), lambda i: (0, 0)),
             pl.BlockSpec((bin_count, block_length), lambda i: (0, 0)),
-            pl.BlockSpec((1, bin_count, 1), lambda i: (i, 0, 0)),
-            pl.BlockSpec((1, bin_count, 1), lambda i: (i, 0, 0)),
+            pl.BlockSpec((bin_count, steps), lambda i: (0, 0)),
+            pl.BlockSpec((bin_count, steps), lambda i: (0, 0)),
             pl.BlockSpec((1, 1, block_length), lambda i: (i, 0, 0)),
             pl.BlockSpec((window_length, width), lambda i: (0, 0)),
         ],

time: 115 us -> 115 us (level)
    unnamed x18 -> x20, local copies, waits for them, and re-layouts: 6.75 us -> 7.27 us
  transfers between devices with their start and end apart: 2 -> 2, of which waited for: 2 -> 2; matrix products, arithmetic and copies ran while one was open for 0% -> 0% of each run, Pallas kernels for 15% -> 14%
where the time goes in v6:
time: 115 us; the launch traced here: 114 us
  Pallas kernels  82.9 us (72%)
  waiting for transfers between devices  16.4 us (14%)
  local copies, waits for them, and re-layouts  7.52 us (7%)
  starting transfers between devices  5.33 us (5%)
    pallas_call x2, Pallas kernels, transform(): pl.pallas_call(functools.partial(dft_kernel, tail, windows), grid=(steps,...  32.6 us
    pallas_call x1, Pallas kernels, gather_pieces(): pl.pallas_call(functools.partial(gather_kernel, time_count, chan_count),...  31.5 us
    pallas_call x1, Pallas kernels, stacked_bands(): pl.pallas_call(gram_kernel, grid=(bins // block,), in_specs=[pl.BlockSpec...  18.9 us
    ppermute x2, waiting for transfers between devices, passed_along(): return lax.ppermute(block, axis, route)  16.4 us
    unnamed x20, local copies, waits for them, and re-layouts  7.27 us
    ppermute x2, starting transfers between devices, passed_along(): return lax.ppermute(block, axis, route)  5.33 us
  transfers between devices with their start and end apart: 2, of which 2 were waited for; matrix products, arithmetic and copies ran while one was open for 0% of the time, Pallas kernels for 14%

profile of v6, /device:TPU:17, one launch (start us, length us, event | category | flops | bytes accessed | tf_op | source)
XLA Modules:
  0.0 114.4 jit_solution(2934595433002634359)
XLA Ops:
  0.0 0.0 copy-start.9
  0.0 0.7 broadcast_subtract_fusion.offsets_ref
  0.7 3.1 %collective-permute-start = (s32[4]{0:T(128)S(1)}, s32[4]{0:T(128)S(1)}, u32[]{:S(2)}, u32[]{:S(2)}) collective-permute-start(s32[4]{0:T(128)S(1)} %broadcast_subtract_fusion.offsets_ref), channel_id=1, source_target_pairs={{0,4},{4,8},{8,12},{12,16},{16,20},{20,24},{24,28},{1,5},{5,9},{9,... | collective-permute-start | bytes 56 | tf_op jit(solution)/shard_map/ppermute | solution.py:25
  3.8 2.1 %collective-permute-done.offsets_ref = s32[4]{0:T(128)S(1)} collective-permute-done((s32[4]{0:T(128)S(1)}, s32[4]{0:T(128)S(1)}, u32[]{:S(2)}, u32[]{:S(2)}) %collective-permute-start) | collective-permute-done | bytes 48 | tf_op jit(solution)/shard_map/ppermute | solution.py:25
  5.8 1.9 %copy-done = bf16[12288,128]{1,0:T(8,128)(2,1)S(1)} copy-done((bf16[12288,128]{1,0:T(8,128)(2,1)S(1)}, bf16[12288,128]{1,0:T(8,128)(2,1)}, u32[]{:S(2)}) %copy-start) | copy-done | bytes 3145752
  7.7 1.4 %copy-done.2 = f32[352,1024]{1,0:T(8,128)S(1)} copy-done((f32[352,1024]{1,0:T(8,128)S(1)}, f32[352,1024]{1,0:T(8,128)}, u32[]{:S(2)}) %copy-start.2) | copy-done | bytes 1441816
  9.1 1.4 %copy-done.4 = f32[352,1024]{1,0:T(8,128)S(1)} copy-done((f32[352,1024]{1,0:T(8,128)S(1)}, f32[352,1024]{1,0:T(8,128)}, u32[]{:S(2)}) %copy-start.4) | copy-done | bytes 1441816
  10.5 0.9 copy-done.5
  11.4 0.9 copy-done.7
  12.3 0.8 copy-done.8
  13.1 16.1 %windowed_transform.3 = f32[704,512]{1,0:T(8,128)S(1)} custom-call(s32[4]{0:T(128)S(1)} %collective-permute-done.offsets_ref, f32[352,1024]{1,0:T(8,128)S(1)} %copy-done.4, f32[352,1024]{1,0:T(8,128)S(1)} %copy-done.2, f32[352,12]{1,0:T(8,128)S(1)} %copy-done.7, f32[352,12]{1,0:T(8,128)S(1)} %copy-done.5, f32[12,1,1024]{2,1,0:T(1,128)S(1)} %copy-done.8, ...), custom_call_target="tpu_custom_call" | custom-call | flops 8858370048 | bytes 3145728 | tf_op jit(solution)/shard_map/windowed_transform/pallas_call | solution.py:94
  29.2 2.2 %collective-permute-start.1 = (f32[704,512]{1,0:T(8,128)S(1)}, f32[704,512]{1,0:T(8,128)S(1)}, u32[]{:S(2)}, u32[]{:S(2)}) collective-permute-start(f32[704,512]{1,0:T(8,128)S(1)} %windowed_transform.3), channel_id=1, source_target_pairs={{4,0},{8,4},{12,8},{16,12},{20,16},{24,20},{28,24},{5,1},{9,5},{13... | collective-permute-start | bytes 4325384 | tf_op jit(solution)/shard_map/ppermute | solution.py:25
  31.4 0.0 copy-done.9
  31.5 0.0 copy-done.1
  31.5 0.0 copy-done.3
  31.5 0.0 copy-done.6
  31.5 16.5 %windowed_transform.2 = f32[704,512]{1,0:T(8,128)S(1)} custom-call(s32[4]{0:T(128)S(1)} %broadcast_subtract_fusion.offsets_ref, f32[352,1024]{1,0:T(8,128)S(1)} %copy-done.4, f32[352,1024]{1,0:T(8,128)S(1)} %copy-done.3, f32[352,12]{1,0:T(8,128)S(1)} %copy-done.7, f32[352,12]{1,0:T(8,128)S(1)} %copy-done.6, f32[12,1,1024]{2,1,0:T(1,128)S(1)} %copy-done.8, ...), custom_call_target="tpu_custom_call" | custom-call | flops 8858370048 | bytes 3145728 | tf_op jit(solution)/shard_map/windowed_transform/pallas_call | solution.py:94
  48.0 14.3 %collective-permute-done.1 = f32[704,512]{1,0:T(8,128)S(1)} collective-permute-done((f32[704,512]{1,0:T(8,128)S(1)}, f32[704,512]{1,0:T(8,128)S(1)}, u32[]{:S(2)}, u32[]{:S(2)}) %collective-permute-start.1) | collective-permute-done | bytes 1441824 | tf_op jit(solution)/shard_map/ppermute | solution.py:25
  62.3 0.3 add.23
  62.7 1.0 fusion.6
  63.7 0.1 pad_maximum_fusion
  63.8 0.3 convert_element_type.10.white_ref
  64.0 31.5 %gather_pieces.1.pieces_ref = bf16[4,8,288,128]{3,2,1,0:T(8,128)(2,1)S(1)} custom-call(bf16[8,288,128]{2,1,0:T(8,128)(2,1)S(1)} %convert_element_type.10.white_ref), custom_call_target="tpu_custom_call" | custom-call | tf_op jit(solution)/shard_map/gather_pieces/pallas_call | solution.py:238
  95.5 18.9 %stacked_bands.1 = f32[2,36,128,512]{3,2,1,0:T(8,128)} custom-call(bf16[4,8,288,128]{3,2,1,0:T(8,128)(2,1)S(1)} %gather_pieces.1.pieces_ref), custom_call_target="tpu_custom_call" | custom-call | tf_op jit(solution)/shard_map/stacked_bands/pallas_call | solution.py:303
  (12 shorter events, 0.0 us)
Async XLA Ops:
  0.0 31.4 %copy-start.9 = (s32[128]{0:T(128)S(1)}, s32[128]{0:T(128)}, u32[]{:S(2)}) copy-start(s32[128]{0:T(128)} %param.15) | copy-start | bytes 1540
  0.7 5.2 %collective-permute-start = (s32[4]{0:T(128)S(1)}, s32[4]{0:T(128)S(1)}, u32[]{:S(2)}, u32[]{:S(2)}) collective-permute-start(s32[4]{0:T(128)S(1)} %broadcast_subtract_fusion.offsets_ref), channel_id=1, source_target_pairs={{0,4},{4,8},{8,12},{12,16},{16,20},{20,24},{24,28},{1,5},{5,9},{9,... | collective-permute-start | bytes 56 | tf_op jit(solution)/shard_map/ppermute | solution.py:25
  5.8 1.9 %copy-start = (bf16[12288,128]{1,0:T(8,128)(2,1)S(1)}, bf16[12288,128]{1,0:T(8,128)(2,1)}, u32[]{:S(2)}) copy-start(bf16[12288,128]{1,0:T(8,128)(2,1)} %refs_5_.3) | copy-start | bytes 9437188
  7.7 1.4 %copy-start.2 = (f32[352,1024]{1,0:T(8,128)S(1)}, f32[352,1024]{1,0:T(8,128)}, u32[]{:S(2)}) copy-start(f32[352,1024]{1,0:T(8,128)} %constant.26.clone.refs_1_) | copy-start | bytes 4325380
  9.1 1.4 %copy-start.4 = (f32[352,1024]{1,0:T(8,128)S(1)}, f32[352,1024]{1,0:T(8,128)}, u32[]{:S(2)}) copy-start(f32[352,1024]{1,0:T(8,128)} %constant.25.clone.refs_0_) | copy-start | bytes 4325380
  10.5 0.9 copy-start.5
  11.4 0.9 copy-start.7
  12.3 0.8 copy-start.8
  13.1 18.4 %copy-start.1 = (bf16[12288,128]{1,0:T(8,128)(2,1)S(1)}, bf16[12288,128]{1,0:T(8,128)(2,1)}, u32[]{:S(2)}) copy-start(bf16[12288,128]{1,0:T(8,128)(2,1)} %refs_5_.3) | copy-start | bytes 9437188
  13.1 18.4 %copy-start.3 = (f32[352,1024]{1,0:T(8,128)S(1)}, f32[352,1024]{1,0:T(8,128)}, u32[]{:S(2)}) copy-start(f32[352,1024]{1,0:T(8,128)} %constant.26.clone.refs_1_) | copy-start | bytes 4325380
  13.1 18.4 %copy-start.6 = (f32[352,12]{1,0:T(8,128)S(1)}, f32[352,12]{1,0:T(8,128)}, u32[]{:S(2)}) copy-start(f32[352,12]{1,0:T(8,128)} %constant.28.clone.refs_3_) | copy-start | bytes 50692
  29.2 33.1 %collective-permute-start.1 = (f32[704,512]{1,0:T(8,128)S(1)}, f32[704,512]{1,0:T(8,128)S(1)}, u32[]{:S(2)}, u32[]{:S(2)}) collective-permute-start(f32[704,512]{1,0:T(8,128)S(1)} %windowed_transform.3), channel_id=1, source_target_pairs={{4,0},{8,4},{12,8},{16,12},{20,16},{24,20},{28,24},{5,1},{9,5},{13... | collective-permute-start | bytes 4325384 | tf_op jit(solution)/shard_map/ppermute | solution.py:25
